TPU v7x, 256 devices: a whole 4x4x8 slice. The times are simulated.
256 devices in a mesh: ctx: 32 (over z, y), head: 8 (over x, core).
Axes of the slice: x: 4, y: 4, z: 8, core: 2. Of those that a mesh axis runs over, the one named last changes fastest.
Arguments:
- prompt_hidden: bfloat16 [16384, 7168], P('ctx', 'head'), may hold values from -6 to 6
- latent_down: bfloat16 [7168, 512], P('head'), may hold values from -0.0625 to 0.0625
- rope_down: bfloat16 [64, 7168], P(None, 'head'), may hold values from -0.0625 to 0.0625
- latent_gain: float32 [512], replicated, may hold values from 0.1 to 1.9
- request_lengths: int32 [4], replicated, may hold values from 1 to 8192, 16384 in all
- row_request: int32 [128], replicated, may hold values from 0 to 3
- query_nope: bfloat16 [4, 128, 128, 128], P(None, 'ctx', 'head'), may hold values from -6 to 6
- query_rope: bfloat16 [4, 128, 128, 64], P(None, 'ctx', 'head'), may hold values from -100 to 100
- new_latent: bfloat16 [4, 128, 512], P(None, 'ctx'), may hold values from -6 to 6
- new_rope: bfloat16 [4, 128, 64], P(None, 'ctx'), may hold values from -4 to 4
- key_up: bfloat16 [128, 128, 512], P('head'), may hold values from -0.5 to 0.5
- value_up: bfloat16 [128, 512, 128], P('head'), may hold values from -0.25 to 0.25
Outputs:
- latent_cache: bfloat16 [16384, 512], P('ctx')
- rope_cache: bfloat16 [64, 16384], P(None, 'ctx')
- head_values: bfloat16 [4, 128, 128, 128], P(None, 'ctx', 'head')
Inputs may be any that keep to these rules, and one draw needn't show every extreme that they name: `request_lengths`: the lengths sum to 16384; the longest is exactly 8192.
All inputs are finite; a program needn't handle non-finite values.
Results may differ from a plain program's by a relative error of at most 0.02.
Values may be sent and summed in bfloat16 or wider, within the bound.
A program may use at most 128 MiB of HBM per device.

v0:
```python
import jax
import jax.numpy as jnp
from jax import lax
from jax.sharding import PartitionSpec as P

epsilon = 1e-06
masked_score = -1e30


def owners(positions, request_lengths):
    end_points = jnp.cumsum(request_lengths, dtype=jnp.int32)
    starts = end_points - request_lengths
    inside = (positions[:, None] >= starts[None, :]) & (positions[:, None] < end_points[None, :])
    numbers = jnp.arange(request_lengths.shape[0], dtype=jnp.int32)
    request_of = jnp.sum(jnp.where(inside, numbers[None, :], 0), axis=1, dtype=jnp.int32)
    offset = positions - jnp.sum(jnp.where(inside, starts[None, :], 0), axis=1, dtype=jnp.int32)
    return (request_of, offset)


def normalize(latent_sum, latent_gain):
    mean_square = jnp.mean(latent_sum * latent_sum, axis=-1, keepdims=True)
    return (latent_sum * lax.rsqrt(mean_square + epsilon) * latent_gain).astype(jnp.bfloat16)


def rotate(rope_rows, offset):
    half_rows = rope_rows.shape[0] // 2
    frequency = 10000.0 ** (-2.0 * jnp.arange(half_rows, dtype=jnp.float32) / rope_rows.shape[0])
    angles = frequency[:, None] * offset.astype(jnp.float32)[None, :]
    cosine = jnp.cos(angles)
    sine_part = jnp.sin(angles)
    leading = rope_rows[:half_rows]
    trailing = rope_rows[half_rows:]
    rotated = jnp.concatenate(
        [leading * cosine - trailing * sine_part, leading * sine_part + trailing * cosine], axis=0
    )
    return rotated.astype(jnp.bfloat16)


def block_weights(scores, allowed):
    block_max = jnp.max(jnp.where(allowed, scores, masked_score), axis=-1)
    weights = jnp.where(allowed, jnp.exp(scores - block_max[..., None]), 0.0)
    return (weights, jnp.sum(weights, axis=-1), block_max)


def local(
    prompt_hidden,
    latent_down,
    rope_down,
    latent_gain,
    request_lengths,
    row_request,
    query_nope,
    query_rope,
    new_latent,
    new_rope,
    key_up,
    value_up,
):
    tok_dev = prompt_hidden.shape[0]
    first_pos = lax.axis_index("ctx") * tok_dev
    part_latent = jnp.dot(prompt_hidden, latent_down, preferred_element_type=jnp.float32)
    part_rope = lax.dot_general(
        rope_down, prompt_hidden, (((1,), (1,)), ((), ())), preferred_element_type=jnp.float32
    )
    full_latent, full_rope = lax.psum((part_latent, part_rope), "head")
    positions = first_pos + jnp.arange(tok_dev, dtype=jnp.int32)
    unused_owner, offset = owners(positions, request_lengths)
    latent_cache = normalize(full_latent, latent_gain)
    rope_cache = rotate(full_rope, offset)
    key_positions = first_pos + jnp.arange(tok_dev, dtype=jnp.int32)
    key_owner, unused_offset = owners(key_positions, request_lengths)
    steps, own_rows, heads_local, nope_width = query_nope.shape
    rope_width = query_rope.shape[-1]
    lat_width = key_up.shape[-1]
    scale = (nope_width + rope_width) ** (-0.5)
    start = lax.axis_index("ctx") * own_rows
    all_nope, all_rope = (
        lax.all_gather(query_nope, "ctx", axis=1, tiled=True),
        lax.all_gather(query_rope, "ctx", axis=1, tiled=True),
    )
    absorbed = jnp.einsum(
        "trhn,hnc->trhc", all_nope, key_up, preferred_element_type=jnp.float32
    ).astype(jnp.bfloat16)
    own_absorbed = lax.dynamic_slice_in_dim(absorbed, start, own_rows, 1)
    all_rows = absorbed.shape[1]
    flat_abs = absorbed.reshape(steps * all_rows, heads_local, lat_width)
    flat_rope = all_rope.reshape(steps * all_rows, heads_local, rope_width)
    scores = (
        jnp.einsum("qhc,kc->qhk", flat_abs, latent_cache, preferred_element_type=jnp.float32)
        + jnp.einsum("qhp,pk->qhk", flat_rope, rope_cache, preferred_element_type=jnp.float32)
    ) * scale
    row_owner = jnp.tile(row_request, steps)
    allowed = (row_owner[:, None] == key_owner[None, :])[:, None, :]
    weights, total, block_max = block_weights(scores, allowed)
    mixed = jnp.einsum(
        "qhk,kc->qhc",
        weights.astype(jnp.bfloat16),
        latent_cache,
        preferred_element_type=jnp.float32,
    )
    lifted = jnp.einsum(
        "qhc,hcv->qhv", mixed.astype(jnp.bfloat16), value_up, preferred_element_type=jnp.float32
    )
    value_width = lifted.shape[-1]
    lifted = lifted.reshape(steps, all_rows, heads_local, value_width)
    total = total.reshape(steps, all_rows, heads_local)
    block_max = block_max.reshape(steps, all_rows, heads_local)
    fresh = (
        jnp.einsum("trhc,krc->trhk", own_absorbed, new_latent, preferred_element_type=jnp.float32)
        + jnp.einsum("trhp,krp->trhk", query_rope, new_rope, preferred_element_type=jnp.float32)
    ) * scale
    step_index = jnp.arange(steps, dtype=jnp.int32)
    causal = (step_index[None, :] <= step_index[:, None])[:, None, None, :]
    fresh_weights, fresh_total, fresh_max = block_weights(fresh, causal)
    fresh_mixed = jnp.einsum(
        "trhk,krc->trhc",
        fresh_weights.astype(jnp.bfloat16),
        new_latent,
        preferred_element_type=jnp.float32,
    )
    fresh_lifted = jnp.einsum(
        "trhc,hcv->trhv",
        fresh_mixed.astype(jnp.bfloat16),
        value_up,
        preferred_element_type=jnp.float32,
    )
    own_max = lax.dynamic_slice_in_dim(block_max, start, own_rows, 1)
    with_fresh = lax.dynamic_update_slice_in_dim(
        block_max, jnp.maximum(own_max, fresh_max), start, 1
    )
    top = lax.pmax(with_fresh.astype(jnp.bfloat16), "ctx").astype(with_fresh.dtype)
    factor = jnp.exp(block_max - top)
    summed_values, summed_total = (
        lax.psum_scatter(
            (lifted * factor[..., None]).astype(jnp.bfloat16),
            "ctx",
            scatter_dimension=1,
            tiled=True,
        ).astype(jnp.float32),
        lax.psum_scatter(
            (total * factor).astype(jnp.bfloat16), "ctx", scatter_dimension=1, tiled=True
        ).astype(jnp.float32),
    )
    top_own = lax.dynamic_slice_in_dim(top, start, own_rows, 1)
    fresh_factor = jnp.exp(fresh_max - top_own)
    numerator = summed_values + fresh_lifted * fresh_factor[..., None]
    denominator = summed_total + fresh_total * fresh_factor
    head_values = (numerator / denominator[..., None]).astype(jnp.bfloat16)
    return (latent_cache, rope_cache, head_values)


def solution(mesh):
    placed = (
        P("ctx", "head"),
        P("head", None),
        P(None, "head"),
        P(),
        P(),
        P(),
        P(None, "ctx", "head", None),
        P(None, "ctx", "head", None),
        P(None, "ctx", None),
        P(None, "ctx", None),
        P("head", None, None),
        P("head", None, None),
    )
    return jax.shard_map(
        local,
        mesh=mesh,
        in_specs=placed,
        out_specs=(P("ctx", None), P(None, "ctx"), P(None, "ctx", "head", None)),
        check_vma=False,
    )
```

profile of v0, /device:TPU:1, one launch (start us, length us, event | category | flops | bytes accessed | tf_op | source)
XLA Modules:
  0.0 589.3 jit_solution(9967902883684103090)
XLA Ops:
  8.0 0.0 all-reduce.4.cloned.1.call-start
  8.1 3.3 fusion.65
  11.4 2.3 fusion.66
  13.7 0.0 all-reduce.4.cloned.1.call-update
  13.7 0.0 all-gather.5.cloned.1.call-start
  13.8 0.5 all-gather.5.cloned.1.call-update
  14.3 0.0 all-gather.3.cloned.1.call-start
  14.3 1.5 copy.90
  15.8 0.0 all-gather.3.cloned.1.call-update
  15.8 0.0 reduce-scatter.2.cloned.1.call-start
  15.9 0.8 reduce-window.8
  16.8 0.7 bitcast_subtract_fusion
  17.4 0.1 select_reduce_fusion.2
  17.5 0.7 broadcast_bitcast_fusion
  18.2 0.2 broadcast_compare_fusion
  18.4 66.1 %all-reduce.4.cloned.1.call-done = (f32[512,512]{1,0:T(8,128)}, f32[64,512]{1,0:T(8,128)}) async-done(((f32[512,512]{1,0:T(8,128)}, f32[64,512]{1,0:T(8,128)}), (f32[512,512]{1,0:T(8,128)}, f32[64,512]{1,0:T(8,128)})) %all-reduce.4.cloned.1.call-update) | async-done | bytes 1179664 | tf_op jit(solution)/shard_map/psum | solution.py:65
  84.5 1.2 fusion.47
  85.7 1.4 multiply_reduce_fusion
  87.1 1.4 multiply_convert_fusion
  88.5 6.1 %all-gather.5.cloned.1.call-done = bf16[4,128,16,64]{3,2,1,0:T(8,128)(2,1)} async-done(((bf16[4,4,16,64]{3,2,1,0:T(8,128)(2,1)}), bf16[4,128,16,64]{3,2,1,0:T(8,128)(2,1)}) %all-gather.5.cloned.1.call-update) | async-done | bytes 1048592 | tf_op jit(solution)/shard_map/all_gather | solution.py:79
  94.6 9.7 %fusion.17 = f32[512,512,16]{1,0,2:T(8,128)} fusion(bf16[512,16,64]{2,1,0:T(8,128)(2,1)} %bitcast.105, bf16[64,512]{1,0:T(8,128)(2,1)S(1)} %pad_maximum_fusion), kind=kOutput, calls=%fused_computation.16 | convolution fusion | flops 536870912 | bytes 17891328 | tf_op jit(solution)/shard_map/qhp,pk->qhk/dot_general | solution.py:90
  104.3 68.0 %all-gather.3.cloned.1.call-done = bf16[4,128,16,128]{3,2,0,1:T(8,128)(2,1)} async-done(((bf16[4,4,16,128]{3,2,0,1:T(8,128)(2,1)}), bf16[4,128,16,128]{3,2,0,1:T(8,128)(2,1)}) %all-gather.3.cloned.1.call-update) | async-done | bytes 2097168 | tf_op jit(solution)/shard_map/all_gather | solution.py:78
  172.3 2.9 copy.91
  175.2 5.6 bitcast_convert_fusion
  180.8 14.8 %select_reduce_fusion = (f32[512,16]{0,1:T(8,128)S(1)}, f32[512,16,512]{0,2,1:T(8,128)}) fusion(pred[512,512]{0,1:T(8,128)(4,1)S(1)} %broadcast_compare_fusion, f32[512,512,16]{1,0,2:T(8,128)} %fusion.17, bf16[512,16,512]{2,0,1:T(8,128)(2,1)} %bitcast.102, bf16[512,512]{1,0:T(8,128)(2,1)S(1)} %multiply_convert_fusion), kind=kOutput, calls=%fused_computation.3 | convolution fusion | flops 4311736320 | bytes 42762240 | tf_op jit(solution)/shard_map/qhc,kc->qhk/dot_general | solution.py:89
  195.6 1.2 dynamic-slice_bitcast_fusion
  196.8 0.4 convolution_bitcast_fusion.1
  197.2 0.3 select_reduce_fusion.1
  197.5 0.1 copy.99
  197.6 0.1 dynamic-slice_maximum_fusion
  197.7 0.2 dynamic_update_slice.3
  197.9 114.3 %pmax.7 = bf16[4,128,16]{1,2,0:T(8,128)(2,1)S(1)} all-reduce(bf16[4,128,16]{1,2,0:T(8,128)(2,1)S(1)} %dynamic_update_slice.3), channel_id=1, replica_groups=mesh['ctx'=32,'head'=8] {'ctx'}, use_global_device_ids=true, to_apply=%region_8.9 | all-reduce | flops 8192 | bytes 32768 | tf_op jit(solution)/shard_map/pmax | solution.py:131
  312.2 8.6 %fusion.1 = f32[512,16]{0,1:T(8,128)S(1)} fusion(f32[512,16,512]{0,2,1:T(8,128)} %get-tuple-element.34, f32[512,16]{0,1:T(8,128)S(1)} %get-tuple-element.33, pred[512,512]{0,1:T(8,128)(4,1)S(1)} %broadcast_compare_fusion), kind=kLoop, calls=%fused_computation.4 | loop fusion | flops 12574720 | bytes 17104896 | tf_op jit(solution)/shard_map/reduce_sum | solution.py:42
  320.9 0.1 copy.102
  321.0 12.4 %fusion.5 = f32[16,512,128]{2,1,0:T(8,128)} fusion(bf16[16,512,128]{2,1,0:T(8,128)(2,1)} %param.23, f32[512,16,512]{0,2,1:T(8,128)} %get-tuple-element.34, f32[512,16]{0,1:T(8,128)S(1)} %get-tuple-element.33, pred[512,512]{0,1:T(8,128)(4,1)S(1)} %broadcast_compare_fusion, bf16[512,512]{1,0:T(8,128)(2,1)S(1)} %multiply_convert_fusion), kind=kOutput, calls=%fused_computation.7 | convolution fusion | flops 5385486336 | bytes 23887872 | tf_op jit(solution)/shard_map/qhc,hcv->qhv/dot_general | solution.py:101
  333.4 6.0 %fusion.10 = bf16[4,128,16,128]{3,2,0,1:T(8,128)(2,1)} fusion(f32[4,128,16,128]{3,1,0,2:T(8,128)} %bitcast.104, f32[4,128,16]{2,0,1:T(4,128)S(1)} %copy.102), kind=kLoop, calls=%fused_computation.13 | loop fusion | flops 2097152 | bytes 6324224 | tf_op jit(solution)/shard_map/convert_element_type | solution.py:135
  339.4 0.0 reduce-scatter.2.cloned.1.call-update
  339.4 0.6 dynamic-slice.4
  340.7 0.1 copy.110
  340.8 110.7 %all-reduce = bf16[4,128,16]{2,0,1:T(4,128)(2,1)S(1)} all-reduce(bf16[4,128,16]{2,0,1:T(4,128)(2,1)S(1)} %copy.110), channel_id=3, replica_groups=mesh['ctx'=32,'head'=8] {'ctx'}, use_global_device_ids=true, to_apply=%region_11.12.clone | all-reduce | flops 8192 | bytes 32768
  451.5 0.1 copy.111
  451.7 0.1 fusion.53
  451.8 0.1 copy.112
  451.9 0.1 multiply_add_fusion
  452.0 0.3 fusion.19
  452.3 126.6 %reduce-scatter.2.cloned.1.call-done = bf16[4,4,16,128]{3,2,0,1:T(8,128)(2,1)} async-done(((bf16[4,128,16,128]{3,2,0,1:T(8,128)(2,1)}), bf16[4,4,16,128]{3,2,0,1:T(8,128)(2,1)}) %reduce-scatter.2.cloned.1.call-update) | async-done | bytes 65552 | tf_op jit(solution)/shard_map/reduce_scatter | solution.py:134
  578.9 2.1 fusion.32
  581.0 0.7 copy.114
  (26 shorter events, 0.1 us)
Async XLA Ops:
  8.0 167.2 %copy-start = (bf16[16,128,512]{2,1,0:T(8,128)(2,1)S(1)}, bf16[16,128,512]{2,1,0:T(8,128)(2,1)}, u32[]{:S(2)}) copy-start(bf16[16,128,512]{2,1,0:T(8,128)(2,1)} %param.22) | copy-start | bytes 6291460
  8.0 76.4 %all-reduce.4.cloned.1.call-start = ((), (), s32[]{:S(2)}) async-start(), calls=%async_computation.4 | async-start | bytes 2359296 | tf_op jit(solution)/shard_map/psum | solution.py:65
  13.7 80.8 %all-gather.5.cloned.1.call-start = ((), (), s32[]{:S(2)}) async-start(), calls=%async_computation.2 | async-start | bytes 2162688 | tf_op jit(solution)/shard_map/all_gather | solution.py:79
  14.3 158.0 %all-gather.3.cloned.1.call-start = ((), (), s32[]{:S(2)}) async-start(), calls=%async_computation.1 | async-start | bytes 2162688 | tf_op jit(solution)/shard_map/all_gather | solution.py:78
  15.8 563.1 %reduce-scatter.2.cloned.1.call-start = ((), (), s32[]{:S(2)}) async-start(), calls=%async_computation.3 | async-start | bytes 2162688 | tf_op jit(solution)/shard_map/reduce_scatter | solution.py:134
  85.7 18.6 %copy-start.2 = (bf16[64,512]{1,0:T(8,128)(2,1)}, bf16[64,512]{1,0:T(8,128)(2,1)S(1)}, u32[]{:S(2)}) copy-start(bf16[64,512]{1,0:T(8,128)(2,1)S(1)} %pad_maximum_fusion) | copy-start | bytes 196612
  88.5 232.5 %copy-start.1 = (bf16[512,512]{1,0:T(8,128)(2,1)}, bf16[512,512]{1,0:T(8,128)(2,1)S(1)}, u32[]{:S(2)}) copy-start(bf16[512,512]{1,0:T(8,128)(2,1)S(1)} %multiply_convert_fusion) | copy-start | bytes 1572868
  180.8 16.0 %copy-start.4 = (bf16[4,4,512]{2,1,0:T(4,128)(2,1)S(1)}, bf16[4,4,512]{2,1,0:T(4,128)(2,1)}, u32[]{:S(2)}) copy-start(bf16[4,4,512]{2,1,0:T(4,128)(2,1)} %param.20) | copy-start | bytes 49156
  180.8 16.5 %copy-start.3 = (bf16[4,4,16,64]{3,2,1,0:T(8,128)(2,1)S(1)}, bf16[4,4,16,64]{3,2,1,0:T(8,128)(2,1)}, u32[]{:S(2)}) copy-start(bf16[4,4,16,64]{3,2,1,0:T(8,128)(2,1)} %param.19) | copy-start | bytes 98308
  180.8 16.5 %copy-start.5 = (bf16[4,4,64]{2,1,0:T(4,128)(2,1)S(1)}, bf16[4,4,64]{2,1,0:T(4,128)(2,1)}, u32[]{:S(2)}) copy-start(bf16[4,4,64]{2,1,0:T(4,128)(2,1)} %param.21) | copy-start | bytes 6148
  333.4 6.0 %copy-start.6 = (u32[256]{0:T(256)S(1)}, u32[256]{0:T(256)}, u32[]{:S(2)}) copy-start(u32[256]{0:T(256)} %constant.45) | copy-start | bytes 3076
Sparse Core Ops, SparseCore 0:
  13.8 70.5 all-reduce.3
Sparse Core Ops, SparseCore 1:
  16.8 77.7 all-gather.4
  97.6 74.6 all-gather.2
  339.5 239.4 reduce-scatter.1
where the time goes:
time: 594 us; the launch traced here: 589 us
  waiting for transfers between devices  267 us (45%)
  blocking collectives  225 us (38%)
  matrix products  51.3 us (9%)
  other arithmetic  20.7 us (3%)
  between operations  16.5 us (3%)
  local copies, waits for them, and re-layouts  8.35 us (1%)
    reduce_scatter x1, waiting for transfers between devices, local(): lax.psum_scatter((lifted * factor[..., None]).astype(jnp.bfloat16), 'ctx'...  127 us
    pmax x1, blocking collectives, local(): lax.pmax(with_fresh.astype(jnp.bfloat16), 'ctx').astype(with_fresh.dtype)  114 us
    unnamed x1, blocking collectives  111 us
    all_gather x1, waiting for transfers between devices, local(): lax.all_gather(query_nope, 'ctx', axis=1, tiled=True)  68 us
    psum x1, waiting for transfers between devices, local(): full_latent, full_rope = lax.psum((part_latent, part_rope), 'head')  66.1 us
    dot_general x1, matrix products, local(): jnp.einsum('qhc,kc->qhk', flat_abs, latent_cache, preferred_element_type=...  14.8 us
    dot_general x1, matrix products, local(): jnp.einsum('qhc,hcv->qhv', mixed.astype(jnp.bfloat16), value_up, preferre...  12.4 us
  transfers between devices with their start and end apart: 4, of which 4 were waited for; matrix products, arithmetic and copies ran while one was open for 3% of the time, Pallas kernels for 0%

commit v1 on v0

v1 whole, which is shorter than its diff:
```python
import functools
import math

import jax
import jax.numpy as jnp
import numpy as np
from jax import lax
from jax.experimental import pallas as pl
from jax.experimental.pallas import tpu as pltpu
from jax.sharding import PartitionSpec as P

MESH = pl.DeviceIdType.MESH
EPSILON = 1e-6
MASKED = -1e30
Y_SIZE = 4
CORES = 2
LANES = 128
F32 = jnp.float32
BF16 = jnp.bfloat16


def nt(a, b):
    return lax.dot_general(a, b, (((1,), (1,)), ((), ())), preferred_element_type=F32)


def nn(a, b):
    return jnp.dot(a, b, preferred_element_type=F32)


def kernel(
    cfg,
    hid_h, ld_h, rd_h, gain_h, lens, rowreq, qn_h, qr_h, nl_h, nr_h, ku_h, vu_h, freq_h,
    lat_o, rope_o, hv_o,
    hid, ld, rd, gain, qn, qr, nl, nr, ku, vu, freq, loc,
    a_snd, a_rcv, part, b_snd, b_rcv, a_sem, b_ssem, b_rsem,
    kv, vt, vut, rope_t, x_ssem, x_rsem, s0_ssem, s0_rsem, s_ssem, s_rsem, y_ssem, y_rsem, o_sem,
    qf, q_snd, qg, qa, nkv, q1_ssem, q1_rsem, n1_ssem, n1_rsem, q2_ssem, q2_rsem,
    ot, ml, u_snd, u_rcv, ml_rcv, u_ssem, u_rsem, m_ssem, m_rsem,
    o_snd, o_rcv, of, hv, h_ssem, h_rsem,
):
    nz, ny, nx, half, sl, lat, heads, hs, tr, rows, steps, group, rope, scale = cfg
    wide = lat + LANES
    ctx = lax.axis_index("ctx")
    head = lax.axis_index("head")
    z, y = ctx // ny, ctx % ny
    x, c = head // CORES, head % CORES

    def dev(zz, yy, xx, cc):
        return (zz * ny + yy, xx * CORES + cc)

    def up(value, by, size):
        return (value + by) % size

    def remote(src, dst, ssem, rsem, device):
        return pltpu.make_async_remote_copy(
            src_ref=src, dst_ref=dst, send_sem=ssem, recv_sem=rsem, device_id=device, device_id_type=MESH
        )

    sibling = dev(z, y, x, 1 - c)
    x_peer = [None] + [dev(z, y, up(x, d, nx), c) for d in range(1, nx)]
    y_peer = [None] + [dev(z, up(y, d, ny), x, c) for d in range(1, ny)]

    y_order = [0, 1] + ([ny - 1] + list(range(2, ny - 1)) if ny > 2 else [])
    y_place = {d: i for i, d in enumerate(y_order)}

    loads = [
        (qn_h, qn),
        (qr_h, qr),
        (hid_h.at[pl.ds(pl.multiple_of((1 - c) * half, half), half)], hid.at[0]),
        (ld_h, ld),
        (rd_h, rd.at[pl.ds(0, rope)]),
        (hid_h.at[pl.ds(pl.multiple_of(c * half, half), half)], hid.at[1]),
        (nl_h, nl),
        (nr_h, nr),
        (gain_h, gain),
        (freq_h, freq),
        (ku_h.at[pl.ds(y * hs, hs)], ku),
        (vu_h.at[pl.ds(y * hs, hs)], vu),
    ]
    loads = [pltpu.make_async_copy(src, dst, loc.at[i]) for i, (src, dst) in enumerate(loads)]
    for load in loads:
        load.start()

    barrier = pltpu.get_barrier_semaphore()
    peers = [sibling] + x_peer[1:] + y_peer[1:] + [dev(up(z, d, nz), y, x, c) for d in range(1, nz)]
    for peer in peers:
        pl.semaphore_signal(barrier, inc=1, device_id=peer, device_id_type=MESH)

    lane = lax.broadcasted_iota(jnp.int32, (tr, LANES), 1)
    row_of = lax.broadcasted_iota(jnp.int32, (tr, LANES), 0) % rows
    request = jnp.zeros((tr, LANES), jnp.int32)
    for r in range(rows):
        request = jnp.where(row_of == r, rowreq[ctx * rows + r], request)
    one_hot = jnp.where(lane - rope == request, 1.0, 0.0)
    qf[1] = jnp.zeros(qf.shape[1:], F32)
    loads[0].wait()
    loads[1].wait()
    qf[0] = qn[...].astype(F32)
    qf[1, :, :, 0:rope] = qr[...].astype(F32)
    for h in range(heads):
        q_snd[h, :, 0:LANES] = qf[0, :, h, :].astype(BF16)
        q_snd[h, :, LANES:] = (qf[1, :, h, :] + one_hot).astype(BF16)
    qg[0, :, y] = q_snd[pl.ds(y * hs, hs)]
    loads[6].wait()
    loads[7].wait()
    nkv[y, :, 0:lat] = nl[...]
    nkv[y, :, lat:] = jnp.zeros((tr, LANES), BF16)
    nkv[y, :, lat : lat + rope] = nr[...]

    rd[pl.ds(rope, LANES - rope)] = jnp.zeros((LANES - rope, rd.shape[1]), BF16)
    for i in (2, 3, 4):
        loads[i].wait()
    a_snd[:, 0:lat] = nn(hid[0], ld[...]).astype(BF16)
    a_snd[:, lat:] = nt(hid[0], rd[...]).astype(BF16)

    pl.semaphore_wait(barrier, len(peers))
    a_copy = remote(a_snd, a_rcv, a_sem.at[0], a_sem.at[1], sibling)
    a_copy.start()
    q1, n1 = [], []
    for d in range(1, ny):
        to = up(y, d, ny)
        q1.append(
            remote(q_snd.at[pl.ds(to * hs, hs)], qg.at[0, :, y], q1_ssem.at[d], q1_rsem.at[d], y_peer[d])
        )
        n1.append(remote(nkv.at[y], nkv.at[y], n1_ssem.at[d], n1_rsem.at[d], y_peer[d]))
    for copy in q1 + n1:
        copy.start()

    loads[5].wait()
    part[:, 0:lat] = nn(hid[1], ld[...])
    part[:, lat:] = nt(hid[1], rd[...])

    for copy in q1:
        copy.wait_recv()

    def z_copy(d):
        return remote(
            qg.at[0], qg.at[d], q2_ssem.at[d], q2_rsem.at[d], dev(up(z, d, nz), y, x, c)
        )

    z_order = [(i + 1) // 2 if i % 2 else (nz - i // 2) % nz for i in range(nz)]
    for d in z_order[1:]:
        z_copy(d).start()

    a_copy.wait_recv()
    part[...] += a_rcv[...].astype(F32)
    b_snd[...] = part[...].astype(BF16).reshape(nx, sl, wide)
    b = [remote(b_snd.at[up(x, d, nx)], b_rcv.at[d], b_ssem.at[d], b_rsem.at[d], x_peer[d]) for d in range(1, nx)]
    for copy in b:
        copy.start()

    loads[11].wait()
    for h in range(hs):
        vut[pl.ds(h * LANES, LANES)] = vu[h].T
    loads[8].wait()
    loads[9].wait()
    position = (ctx * (half * CORES) + c * half + x * sl) + lax.broadcasted_iota(jnp.int32, (sl, LANES), 0)
    owner = jnp.zeros((sl, LANES), jnp.int32)
    start = jnp.zeros((sl, LANES), jnp.int32)
    end = jnp.int32(0)
    for r in range(lens.shape[0] - 1):
        end = end + lens[r]
        owner = owner + jnp.where(position >= end, 1, 0)
        start = jnp.where(position >= end, end, start)
    angle = freq[...] * (position - start).astype(F32)
    cosine, sine = jnp.cos(angle), jnp.sin(angle)
    lane = lax.broadcasted_iota(jnp.int32, (sl, LANES), 1)
    penalty = jnp.where((lane >= rope) & (lane < rope + lens.shape[0]) & (lane - rope != owner), MASKED, 0.0)

    own_rows = pl.ds(pl.multiple_of(x * sl, sl), sl)
    total = part[own_rows, :]
    for d in range(1, nx):
        b[d - 1].wait_recv()
        total = total + b_rcv[d].astype(F32)
    latent = total[:, 0:lat]
    mean_square = jnp.mean(latent * latent, axis=-1, keepdims=True)
    kv[0, 0, own_rows, 0:lat] = (latent * lax.rsqrt(mean_square + EPSILON) * gain[...]).astype(BF16)
    raw = total[:, lat:]
    turned = jnp.where(lane < rope // 2, -pltpu.roll(raw, LANES - rope // 2, 1), pltpu.roll(raw, rope // 2, 1))
    rotated = jnp.where(lane < rope, raw * cosine + turned * sine, penalty)
    kv[0, 0, own_rows, lat:] = rotated.astype(BF16)

    def x_copy(d):
        place = kv.at[0, 0, own_rows]
        return remote(place, place, x_ssem.at[d], x_rsem.at[d], x_peer[d])

    def to_sibling(d):
        part_rows = pl.ds(pl.multiple_of(up(x, nx - d, nx) * sl, sl), sl)
        return remote(kv.at[0, 0, part_rows], kv.at[1, 0, part_rows], s0_ssem.at[d], s0_rsem.at[d], sibling)

    def y_copy(d, e):
        part_rows = pl.ds(pl.multiple_of(up(x, nx - e, nx) * sl, sl), sl)
        return remote(
            kv.at[0, 0, part_rows], kv.at[0, y_place[d], part_rows], y_ssem.at[d, e], y_rsem.at[d, e], y_peer[d]
        )

    for d in range(1, nx):
        x_copy(d).start()
    to_sibling(0).start()
    for d in y_order[1:]:
        y_copy(d, 0).start()
    for e in range(1, nx):
        x_copy(e).wait_recv()
        to_sibling(e).start()
        for d in y_order[1:]:
            y_copy(d, e).start()

    ml[...] = jnp.zeros(ml.shape, F32)
    for copy in n1:
        copy.wait_recv()
    loads[10].wait()
    for e in range(nx):
        to_sibling(e).wait_recv()

    def chunk_keys(pieces):
        return jnp.concatenate([kv[i, j] for i, j in pieces], axis=0)

    def first_chunk(keys, s):
        qa[s, :, lat:] = qg[s, :, :, :, LANES:].reshape(group, LANES)
        for h in range(hs):
            qa[s, pl.ds(h * (group // hs), group // hs), 0:lat] = nn(
                qg[s, h, :, :, 0:LANES].reshape(group // hs, LANES), ku[h]
            ).astype(BF16)
        scores = nt(keys, qa[s])
        top = jnp.max(scores, axis=0, keepdims=True)
        weights = jnp.exp2((scores - top) * scale)
        ml[s, 0:1, :] = top
        ml[s, 1:2, :] = jnp.sum(weights, axis=0, keepdims=True)
        ot[s] = nn(vt[...], weights.astype(BF16))

    def next_chunk(scores, values, s):
        before = ml[s, 0:1, :]
        top = jnp.maximum(before, jnp.max(scores, axis=0, keepdims=True))
        weights = jnp.exp2((scores - top) * scale)
        keep = jnp.exp2((before - top) * scale)
        ml[s, 0:1, :] = top
        ml[s, 1:2, :] = ml[s, 1:2, :] * keep + jnp.sum(weights, axis=0, keepdims=True)
        return ot[s] * keep + nn(values, weights.astype(BF16))

    pieces = [(0, 0), (1, 0)]
    keys0 = chunk_keys(pieces)
    vt[...] = keys0[:, 0:lat].T

    def visit_first(i, carry):
        s = jnp.where(i % 2 == 1, (i + 1) // 2, (nz - i // 2) % nz)

        @pl.when(i > 0)
        def _():
            z_copy(s).wait_recv()

        first_chunk(chunk_keys([(0, 0), (1, 0)]), s)
        return carry

    lax.fori_loop(0, nz, visit_first, 0)

    sides = [c, 1 - c]
    outs = []
    for i in range(CORES):
        rope_t[i] = kv[i, 0, :, lat:].astype(F32).T[0:rope].astype(BF16)
        place = pl.ds(pl.multiple_of(sides[i] * half, half), half)
        outs.append(pltpu.make_async_copy(kv.at[i, 0, :, pl.ds(0, lat)], lat_o.at[place], o_sem.at[2 * i]))
        outs.append(pltpu.make_async_copy(rope_t.at[i], rope_o.at[:, place], o_sem.at[2 * i + 1]))
    for copy in outs:
        copy.start()

    fresh = ny * tr
    new_keys = nkv[...].reshape(fresh, wide)
    key_of = lax.broadcasted_iota(jnp.int32, (fresh, group), 0)
    query_of = lax.broadcasted_iota(jnp.int32, (fresh, group), 1) % fresh
    allowed = (
        (key_of // tr == query_of // tr)
        & (key_of % rows == query_of % rows)
        & ((key_of % tr) // rows <= (query_of % tr) // rows)
    )
    scores = jnp.where(allowed, nt(new_keys, qa[0]), MASKED)
    ot[0] = next_chunk(scores, new_keys[:, 0:lat].astype(F32).T.astype(BF16), 0)

    def arrive(p):
        for e in range(nx):
            y_copy(y_order[p], e).wait_recv()
        copy = remote(kv.at[0, p], kv.at[1, p], s_ssem.at[p], s_rsem.at[p], sibling)
        copy.start()
        return copy

    forwards = {}
    chunks = []
    if ny > 2:
        chunks = [[(0, 1), (0, 2)], [(1, 1), (1, 2)]]
    chunks += [[(0, p), (1, p)] for p in (range(3, ny) if ny > 2 else range(1, ny))]
    for number, pieces in enumerate(chunks):
        last = number == len(chunks) - 1
        for i, p in pieces:
            if p not in forwards:
                forwards[p] = arrive(p)
        for i, p in pieces:
            if i == 1:
                forwards[p].wait_recv()
        vt[...] = chunk_keys(pieces)[:, 0:lat].T
        if not last:

            def visit(i, carry, pieces=pieces):
                ot[i] = next_chunk(nt(chunk_keys(pieces), qa[i]), vt[...], i)
                return carry

            lax.fori_loop(0, nz, visit, 0)

    def lifted(s, pieces):
        mixed = next_chunk(nt(chunk_keys(pieces), qa[s]), vt[...], s).astype(BF16)
        wide_values = nn(vut[...], mixed)
        of_head = lax.broadcasted_iota(jnp.int32, (LANES, group), 1) // (group // hs)
        values = jnp.zeros((LANES, group), F32)
        for h in range(hs):
            values = jnp.where(of_head == h, wide_values[h * LANES : (h + 1) * LANES], values)
        return values

    def back(s):
        to = dev(up(z, nz - s, nz), y, x, c)
        return (
            remote(u_snd.at[s], u_rcv.at[s], u_ssem.at[s], u_rsem.at[s], to),
            remote(ml.at[s], ml_rcv.at[s], m_ssem.at[s], m_rsem.at[s], to),
        )

    def visit_last(i, carry):
        j = nz - 1 - i
        s = jnp.where(j % 2 == 1, (j + 1) // 2, (nz - j // 2) % nz)
        u_snd[s] = lifted(s, chunks[-1]).astype(BF16)
        for copy in back(s):
            copy.start()
        return carry

    lax.fori_loop(0, nz - 1, visit_last, 0)
    own_values = lifted(0, chunks[-1])

    top = ml[0, 0:1, :]
    for s in range(1, nz):
        for copy in back(s):
            copy.wait_recv()
        top = jnp.maximum(top, ml_rcv[s, 0:1, :])
    keep = jnp.exp2((ml[0, 0:1, :] - top) * scale)
    numerator = own_values * keep
    denominator = ml[0, 1:2, :] * keep
    for s in range(1, nz):
        keep = jnp.exp2((ml_rcv[s, 0:1, :] - top) * scale)
        numerator = numerator + u_rcv[s].astype(F32) * keep
        denominator = denominator + ml_rcv[s, 1:2, :] * keep
    values = (numerator / denominator).T.astype(BF16)
    o_snd[...] = values.reshape(hs, ny, tr, LANES)
    own_heads = pl.ds(y * hs, hs)
    back_y = [
        remote(o_snd.at[:, up(y, d, ny)], o_rcv.at[own_heads], h_ssem.at[d], h_rsem.at[d], y_peer[d])
        for d in range(1, ny)
    ]
    for copy in back_y:
        copy.start()
    o_rcv[own_heads] = o_snd[:, y]
    for copy in back_y:
        copy.wait_recv()
    for h in range(heads):
        of[:, h, :] = o_rcv[h].astype(F32)
    hv[...] = of[...].astype(BF16)
    hv_copy = pltpu.make_async_copy(hv, hv_o, o_sem.at[2 * CORES])
    hv_copy.start()

    a_copy.wait_send()
    for copy in q1 + n1 + b + back_y:
        copy.wait_send()
    for d in range(1, nz):
        z_copy(d).wait_send()
        for copy in back(d):
            copy.wait_send()
    for e in range(nx):
        if e:
            x_copy(e).wait_send()
        to_sibling(e).wait_send()
        for d in range(1, ny):
            y_copy(d, e).wait_send()
    for copy in forwards.values():
        copy.wait_send()
    for copy in outs:
        copy.wait()
    hv_copy.wait()


def local(
    prompt_hidden,
    latent_down,
    rope_down,
    latent_gain,
    request_lengths,
    row_request,
    query_nope,
    query_rope,
    new_latent,
    new_rope,
    key_up,
    value_up,
):
    ny = Y_SIZE
    nz = lax.axis_size("ctx") // ny
    nx = lax.axis_size("head") // CORES
    tok, depth = prompt_hidden.shape
    half = tok // CORES
    sl = half // nx
    steps, rows, heads, nope = query_nope.shape
    rope = query_rope.shape[-1]
    lat = key_up.shape[-1]
    tr = steps * rows
    hs = heads // ny
    group = hs * ny * tr
    wide = lat + LANES
    scale = math.log2(math.e) / math.sqrt(nope + rope)
    cfg = (nz, ny, nx, half, sl, lat, heads, hs, tr, rows, steps, group, rope, scale)
    spare = np.zeros((1, LANES), np.float32)
    frequency = 10000.0 ** (-2.0 * np.arange(rope // 2, dtype=np.float32) / rope)
    spare[0, :rope] = np.tile(frequency.astype(np.float32), 2)
    dma = pltpu.SemaphoreType.DMA
    vmem = pltpu.VMEM
    scratch = [
        vmem((2, half, depth), BF16),
        vmem((depth, lat), BF16),
        vmem((LANES, depth), BF16),
        vmem((1, lat), F32),
        vmem((tr, heads, nope), BF16),
        vmem((tr, heads, rope), BF16),
        vmem((tr, lat), BF16),
        vmem((tr, rope), BF16),
        vmem((hs, nope, lat), BF16),
        vmem((hs, lat, LANES), BF16),
        vmem((1, LANES), F32),
        dma((12,)),
        vmem((half, wide), BF16),
        vmem((half, wide), BF16),
        vmem((half, wide), F32),
        vmem((nx, sl, wide), BF16),
        vmem((nx, sl, wide), BF16),
        dma((2,)),
        dma((nx,)),
        dma((nx,)),
        vmem((CORES, ny, half, wide), BF16),
        vmem((lat, tok), BF16),
        vmem((hs * LANES, lat), BF16),
        vmem((CORES, rope, half), BF16),
        dma((nx,)),
        dma((nx,)),
        dma((nx,)),
        dma((nx,)),
        dma((ny,)),
        dma((ny,)),
        dma((ny, nx)),
        dma((ny, nx)),
        dma((2 * CORES + 1,)),
        vmem((2, tr, heads, LANES), F32),
        vmem((heads, tr, 2 * LANES), BF16),
        vmem((nz, hs, ny, tr, 2 * LANES), BF16),
        vmem((nz, group, wide), BF16),
        vmem((ny, tr, wide), BF16),
        dma((ny,)),
        dma((ny,)),
        dma((ny,)),
        dma((ny,)),
        dma((nz,)),
        dma((nz,)),
        vmem((nz, lat, group), F32),
        vmem((nz, 8, group), F32),
        vmem((nz, LANES, group), BF16),
        vmem((nz, LANES, group), BF16),
        vmem((nz, 8, group), F32),
        dma((nz,)),
        dma((nz,)),
        dma((nz,)),
        dma((nz,)),
        vmem((hs, ny, tr, LANES), BF16),
        vmem((heads, tr, LANES), BF16),
        vmem((tr, heads, LANES), F32),
        vmem((tr, heads, LANES), BF16),
        dma((ny,)),
        dma((ny,)),
    ]
    anywhere = pl.BlockSpec(memory_space=pl.ANY)
    scalars = pl.BlockSpec(memory_space=pltpu.SMEM)
    latent_cache, rope_cache, head_values = pl.pallas_call(
        functools.partial(kernel, cfg),
        out_shape=(
            jax.ShapeDtypeStruct((tok, lat), BF16),
            jax.ShapeDtypeStruct((rope, tok), BF16),
            jax.ShapeDtypeStruct((tr, heads, LANES), BF16),
        ),
        in_specs=[anywhere] * 4 + [scalars] * 2 + [anywhere] * 7,
        out_specs=(anywhere,) * 3,
        scratch_shapes=scratch,
        compiler_params=pltpu.CompilerParams(
            collective_id=0, has_side_effects=True, vmem_limit_bytes=50 * 1024 * 1024
        ),
    )(
        prompt_hidden,
        latent_down,
        rope_down,
        latent_gain.reshape(1, lat),
        request_lengths,
        row_request,
        query_nope.reshape(tr, heads, nope),
        query_rope.reshape(tr, heads, rope),
        new_latent.reshape(tr, lat),
        new_rope.reshape(tr, rope),
        key_up,
        value_up,
        jnp.asarray(spare),
    )
    return (latent_cache, rope_cache, head_values.reshape(steps, rows, heads, LANES))


def solution(mesh):
    placed = (
        P("ctx", "head"),
        P("head", None),
        P(None, "head"),
        P(),
        P(),
        P(),
        P(None, "ctx", "head", None),
        P(None, "ctx", "head", None),
        P(None, "ctx", None),
        P(None, "ctx", None),
        P("head", None, None),
        P("head", None, None),
    )
    return jax.shard_map(
        local,
        mesh=mesh,
        in_specs=placed,
        out_specs=(P("ctx", None), P(None, "ctx"), P(None, "ctx", "head", None)),
        check_vma=False,
    )
```

time: 594 us -> 91.8 us (0.15)
  waiting for transfers between devices: 267 us -> 0 us
  blocking collectives: 225 us -> 0 us
  Pallas kernels: 0 us -> 79.7 us
  matrix products: 51.3 us -> 0 us
  other arithmetic: 20.7 us -> 0 us
  between operations: 16.5 us -> 0.65 us
    reduce_scatter x1 -> x0, waiting for transfers between devices: 127 us -> none  [local(): lax.psum_scatter((lifted * factor[..., None]).astype(jnp.bfloat16), 'ctx'...]
    pmax x1 -> x0, blocking collectives: 114 us -> none  [local(): lax.pmax(with_fresh.astype(jnp.bfloat16), 'ctx').astype(with_fresh.dtype)]
    unnamed x1 -> x0, blocking collectives: 111 us -> none
    pallas_call x0 -> x1, Pallas kernels: none -> 79.7 us  [local(): pl.pallas_call(functools.partial(kernel, cfg), out_shape=(jax.ShapeDtypeS...]
    all_gather x2 -> x0, waiting for transfers between devices: 74 us -> none  [the longest x1 68 us: local(): lax.all_gather(query_nope, 'ctx', axis=1, tiled=True)]
    psum x1 -> x0, waiting for transfers between devices: 66.1 us -> none  [local(): full_latent, full_rope = lax.psum((part_latent, part_rope), 'head')]
    dot_general x9 -> x0, matrix products: 45.7 us -> none  [the longest x1 14.8 us: local(): jnp.einsum('qhc,kc->qhk', flat_abs, latent_cache, preferred_element_type=...]
    reduce_sum x4 -> x0, other arithmetic: 10.2 us -> none  [the longest x2 8.72 us: block_weights(): return (weights, jnp.sum(weights, axis=-1), block_max)]
  transfers between devices with their start and end apart: 4 -> 0, of which waited for: 4 -> 0; matrix products, arithmetic and copies ran while one was open for 3% -> 0% of each run, Pallas kernels for 0% -> 0%
where the time goes in v1:
time: 91.8 us; the launch traced here: 91.4 us
  Pallas kernels  79.7 us (87%)
  local copies, waits for them, and re-layouts  11 us (12%)
    pallas_call x1, Pallas kernels, local(): pl.pallas_call(functools.partial(kernel, cfg), out_shape=(jax.ShapeDtypeS...  79.7 us
    unnamed x23, local copies, waits for them, and re-layouts  10.3 us

profile of v1, /device:TPU:1, one launch (start us, length us, event | category | flops | bytes accessed | tf_op | source)
XLA Modules:
  0.0 91.4 jit_solution(7827750050824517459)
XLA Ops:
  0.6 0.7 reshape.27.nl_h
  1.4 0.0 copy-start
  1.4 1.2 %copy-done = bf16[512,896]{1,0:T(8,128)(2,1)S(1)} copy-done((bf16[512,896]{1,0:T(8,128)(2,1)S(1)}, bf16[512,896]{1,0:T(8,128)(2,1)}, u32[]{:S(2)}) %copy-start) | copy-done | bytes 917528
  2.5 0.0 copy-start.1
  2.5 1.2 %copy-done.1 = bf16[896,512]{1,0:T(8,128)(2,1)S(1)} copy-done((bf16[896,512]{1,0:T(8,128)(2,1)S(1)}, bf16[896,512]{1,0:T(8,128)(2,1)}, u32[]{:S(2)}) %copy-start.1) | copy-done | bytes 917528
  3.7 0.0 copy-start.2
  3.7 0.9 copy-done.2
  4.6 0.0 copy-start.3
  4.6 0.8 copy-done.3
  5.5 0.0 copy-start.4
  5.5 0.8 copy-done.4
  6.3 0.0 copy-start.5
  6.3 0.7 copy-done.5
  7.0 0.0 copy-start.6
  7.0 0.7 copy-done.6
  7.7 0.0 copy-start.7
  7.7 0.7 copy-done.7
  8.3 0.0 copy-start.8
  8.3 0.7 copy-done.8
  9.0 0.0 copy-start.9
  9.0 0.7 copy-done.9
  9.6 79.7 %shard_map.148 = (bf16[512,512]{1,0:T(8,128)(2,1)S(1)}, bf16[64,512]{1,0:T(8,128)(2,1)S(1)}, bf16[16,16,128]{2,1,0:T(8,128)(2,1)S(1)}) custom-call(bf16[512,896]{1,0:T(8,128)(2,1)S(1)} %copy-done, bf16[896,512]{1,0:T(8,128)(2,1)S(1)} %copy-done.1, bf16[64,896]{1,0:T(8,128)(2,1)S(1)} %copy-done.2, f32[1,512]{1,0:T(1,128)S(1)} %bitcast.9, s32[4]{0:T(128)S(1)} %copy-done.7, ...), custom_call_target="tpu_custom_call" | custom-call | tf_op jit(solution)/shard_map/pallas_call | solution.py:481
  89.4 0.8 copy.19
  90.2 0.6 copy.20
  90.8 0.6 copy.21
Async XLA Ops:
  1.4 1.2 %copy-start = (bf16[512,896]{1,0:T(8,128)(2,1)S(1)}, bf16[512,896]{1,0:T(8,128)(2,1)}, u32[]{:S(2)}) copy-start(bf16[512,896]{1,0:T(8,128)(2,1)} %hid_h.1) | copy-start | bytes 2752516
  2.5 1.2 %copy-start.1 = (bf16[896,512]{1,0:T(8,128)(2,1)S(1)}, bf16[896,512]{1,0:T(8,128)(2,1)}, u32[]{:S(2)}) copy-start(bf16[896,512]{1,0:T(8,128)(2,1)} %ld_h.1) | copy-start | bytes 2752516
  3.7 0.9 copy-start.2
  4.6 0.8 copy-start.3
  5.5 0.8 copy-start.4
  6.3 0.7 copy-start.5
  7.0 0.7 copy-start.6
  7.7 0.7 copy-start.7
  8.3 0.7 copy-start.8
  9.0 0.7 copy-start.9

commit v2 on v1

--- a/solution.py
+++ b/solution.py
@@ -15,6 +15,7 @@
 Y_SIZE = 4
 CORES = 2
 LANES = 128
+AT_ONCE = 4
 F32 = jnp.float32
 BF16 = jnp.bfloat16
 
@@ -103,9 +104,9 @@
     qg[0, :, y] = q_snd[pl.ds(y * hs, hs)]
     loads[6].wait()
     loads[7].wait()
-    nkv[y, :, 0:lat] = nl[...]
+    nkv[y, :, 0:lat] = nl[...].reshape(tr, lat)
     nkv[y, :, lat:] = jnp.zeros((tr, LANES), BF16)
-    nkv[y, :, lat : lat + rope] = nr[...]
+    nkv[y, :, lat : lat + rope] = nr[...].reshape(tr, rope)
 
     rd[pl.ds(rope, LANES - rope)] = jnp.zeros((LANES - rope, rd.shape[1]), BF16)
     for i in (2, 3, 4):
@@ -215,43 +216,56 @@
     def chunk_keys(pieces):
         return jnp.concatenate([kv[i, j] for i, j in pieces], axis=0)
 
-    def first_chunk(keys, s):
+    def transpose_values(pieces):
+        for k, (i, j) in enumerate(pieces):
+            vt[:, k * half : (k + 1) * half] = kv[i, j, :, 0:lat].T
+
+    def absorb(s):
         qa[s, :, lat:] = qg[s, :, :, :, LANES:].reshape(group, LANES)
         for h in range(hs):
             qa[s, pl.ds(h * (group // hs), group // hs), 0:lat] = nn(
                 qg[s, h, :, :, 0:LANES].reshape(group // hs, LANES), ku[h]
             ).astype(BF16)
-        scores = nt(keys, qa[s])
-        top = jnp.max(scores, axis=0, keepdims=True)
-        weights = jnp.exp2((scores - top) * scale)
-        ml[s, 0:1, :] = top
-        ml[s, 1:2, :] = jnp.sum(weights, axis=0, keepdims=True)
-        ot[s] = nn(vt[...], weights.astype(BF16))
-
-    def next_chunk(scores, values, s):
-        before = ml[s, 0:1, :]
-        top = jnp.maximum(before, jnp.max(scores, axis=0, keepdims=True))
-        weights = jnp.exp2((scores - top) * scale)
-        keep = jnp.exp2((before - top) * scale)
-        ml[s, 0:1, :] = top
-        ml[s, 1:2, :] = ml[s, 1:2, :] * keep + jnp.sum(weights, axis=0, keepdims=True)
-        return ot[s] * keep + nn(values, weights.astype(BF16))
-
-    pieces = [(0, 0), (1, 0)]
-    keys0 = chunk_keys(pieces)
-    vt[...] = keys0[:, 0:lat].T
-
-    def visit_first(i, carry):
-        s = jnp.where(i % 2 == 1, (i + 1) // 2, (nz - i // 2) % nz)
-
-        @pl.when(i > 0)
-        def _():
-            z_copy(s).wait_recv()
-
-        first_chunk(chunk_keys([(0, 0), (1, 0)]), s)
-        return carry
-
-    lax.fori_loop(0, nz, visit_first, 0)
+
+    def first_keys(keys, values, slots):
+        scores = [nt(keys, qa[s]) for s in slots]
+        tops = [jnp.max(score, axis=0, keepdims=True) for score in scores]
+        weights = [jnp.exp2((score - top) * scale) for score, top in zip(scores, tops)]
+        sums = [jnp.sum(weight, axis=0, keepdims=True) for weight in weights]
+        mixed = [nn(values, weight.astype(BF16)) for weight in weights]
+        return tops, sums, mixed
+
+    def next_keys(scores, values, slots):
+        before = [ml[s, 0:1, :] for s in slots]
+        sums = [ml[s, 1:2, :] for s in slots]
+        tops = [jnp.maximum(old, jnp.max(score, axis=0, keepdims=True)) for old, score in zip(before, scores)]
+        weights = [jnp.exp2((score - top) * scale) for score, top in zip(scores, tops)]
+        keeps = [jnp.exp2((old - top) * scale) for old, top in zip(before, tops)]
+        sums = [
+            old * keep + jnp.sum(weight, axis=0, keepdims=True) for old, keep, weight in zip(sums, keeps, weights)
+        ]
+        mixed = [
+            ot[s] * keep + nn(values, weight.astype(BF16)) for s, keep, weight in zip(slots, keeps, weights)
+        ]
+        return tops, sums, mixed
+
+    def put(slots, tops, sums, mixed):
+        for s, top, total, mix in zip(slots, tops, sums, mixed):
+            ml[s, 0:1, :] = top
+            ml[s, 1:2, :] = total
+            if mix is not None:
+                ot[s] = mix
+
+    at_once = min(AT_ONCE, nz)
+    bunches = [z_order[i : i + at_once] for i in range(0, nz, at_once)]
+    own_pieces = [(0, 0), (1, 0)]
+    transpose_values(own_pieces)
+    for slots in bunches:
+        for s in slots:
+            if s:
+                z_copy(s).wait_recv()
+            absorb(s)
+        put(slots, *first_keys(chunk_keys(own_pieces), vt[:, 0 : CORES * half], slots))
 
     sides = [c, 1 - c]
     outs = []
@@ -273,7 +287,7 @@
         & ((key_of % tr) // rows <= (query_of % tr) // rows)
     )
     scores = jnp.where(allowed, nt(new_keys, qa[0]), MASKED)
-    ot[0] = next_chunk(scores, new_keys[:, 0:lat].astype(F32).T.astype(BF16), 0)
+    put([0], *next_keys([scores], new_keys[:, 0:lat].astype(F32).T.astype(BF16), [0]))
 
     def arrive(p):
         for e in range(nx):
@@ -285,33 +299,19 @@
     forwards = {}
     chunks = []
     if ny > 2:
-        chunks = [[(0, 1), (0, 2)], [(1, 1), (1, 2)]]
+        chunks = [[(0, 1), (0, 2), (1, 1), (1, 2)]]
     chunks += [[(0, p), (1, p)] for p in (range(3, ny) if ny > 2 else range(1, ny))]
-    for number, pieces in enumerate(chunks):
-        last = number == len(chunks) - 1
+    for pieces in chunks[:-1]:
         for i, p in pieces:
             if p not in forwards:
                 forwards[p] = arrive(p)
         for i, p in pieces:
             if i == 1:
                 forwards[p].wait_recv()
-        vt[...] = chunk_keys(pieces)[:, 0:lat].T
-        if not last:
-
-            def visit(i, carry, pieces=pieces):
-                ot[i] = next_chunk(nt(chunk_keys(pieces), qa[i]), vt[...], i)
-                return carry
-
-            lax.fori_loop(0, nz, visit, 0)
-
-    def lifted(s, pieces):
-        mixed = next_chunk(nt(chunk_keys(pieces), qa[s]), vt[...], s).astype(BF16)
-        wide_values = nn(vut[...], mixed)
-        of_head = lax.broadcasted_iota(jnp.int32, (LANES, group), 1) // (group // hs)
-        values = jnp.zeros((LANES, group), F32)
-        for h in range(hs):
-            values = jnp.where(of_head == h, wide_values[h * LANES : (h + 1) * LANES], values)
-        return values
+        transpose_values(pieces)
+        for slots in bunches:
+            keys = chunk_keys(pieces)
+            put(slots, *next_keys([nt(keys, qa[s]) for s in slots], vt[:, 0 : len(pieces) * half], slots))
 
     def back(s):
         to = dev(up(z, nz - s, nz), y, x, c)
@@ -320,16 +320,34 @@
             remote(ml.at[s], ml_rcv.at[s], m_ssem.at[s], m_rsem.at[s], to),
         )
 
-    def visit_last(i, carry):
-        j = nz - 1 - i
-        s = jnp.where(j % 2 == 1, (j + 1) // 2, (nz - j // 2) % nz)
-        u_snd[s] = lifted(s, chunks[-1]).astype(BF16)
-        for copy in back(s):
-            copy.start()
-        return carry
-
-    lax.fori_loop(0, nz - 1, visit_last, 0)
-    own_values = lifted(0, chunks[-1])
+    pieces = chunks[-1]
+    for i, p in pieces:
+        if p not in forwards:
+            forwards[p] = arrive(p)
+    for i, p in pieces:
+        if i == 1:
+            forwards[p].wait_recv()
+    transpose_values(pieces)
+    of_head = lax.broadcasted_iota(jnp.int32, (LANES, group), 1) // (group // hs)
+    own_values = None
+    for slots in bunches[::-1]:
+        slots = slots[::-1]
+        keys = chunk_keys(pieces)
+        tops, sums, mixed = next_keys([nt(keys, qa[s]) for s in slots], vt[:, 0 : len(pieces) * half], slots)
+        put(slots, tops, sums, [None] * len(slots))
+        for s, mix in zip(slots, mixed):
+            every = nn(vut[...], mix.astype(BF16))
+            values = every[0:LANES]
+            for h in range(1, hs):
+                values = jnp.where(of_head == h, every[h * LANES : (h + 1) * LANES], values)
+            if s:
+                u_snd[s] = values.astype(BF16)
+            else:
+                own_values = values
+        for s in slots:
+            if s:
+                for copy in back(s):
+                    copy.start()
 
     top = ml[0, 0:1, :]
     for s in range(1, nz):
@@ -422,8 +440,8 @@
         vmem((1, lat), F32),
         vmem((tr, heads, nope), BF16),
         vmem((tr, heads, rope), BF16),
-        vmem((tr, lat), BF16),
-        vmem((tr, rope), BF16),
+        vmem((steps, rows, lat), BF16),
+        vmem((steps, rows, rope), BF16),
         vmem((hs, nope, lat), BF16),
         vmem((hs, lat, LANES), BF16),
         vmem((1, LANES), F32),
@@ -437,7 +455,7 @@
         dma((nx,)),
         dma((nx,)),
         vmem((CORES, ny, half, wide), BF16),
-        vmem((lat, tok), BF16),
+        vmem((lat, max(1, ny // 2) * tok), BF16),
         vmem((hs * LANES, lat), BF16),
         vmem((CORES, rope, half), BF16),
         dma((nx,)),
@@ -489,7 +507,7 @@
         out_specs=(anywhere,) * 3,
         scratch_shapes=scratch,
         compiler_params=pltpu.CompilerParams(
-            collective_id=0, has_side_effects=True, vmem_limit_bytes=50 * 1024 * 1024
+            collective_id=0, has_side_effects=True, vmem_limit_bytes=60 * 1024 * 1024
         ),
     )(
         prompt_hidden,
@@ -500,8 +518,8 @@
         row_request,
         query_nope.reshape(tr, heads, nope),
         query_rope.reshape(tr, heads, rope),
-        new_latent.reshape(tr, lat),
-        new_rope.reshape(tr, rope),
+        new_latent,
+        new_rope,
         key_up,
         value_up,
         jnp.asarray(spare),

time: 91.8 us -> 77.7 us (0.85)
  Pallas kernels: 79.7 us -> 71.1 us
  local copies, waits for them, and re-layouts: 11 us -> 4.81 us
    pallas_call x1, Pallas kernels: 79.7 us -> 71.1 us  [local(): pl.pallas_call(functools.partial(kernel, cfg), out_shape=(jax.ShapeDtypeS...]
    unnamed x23 -> x3, local copies, waits for them, and re-layouts: 10.3 us -> 4.81 us
where the time goes in v2:
time: 77.7 us; the launch traced here: 76.5 us
  Pallas kernels  71.1 us (92%)
  local copies, waits for them, and re-layouts  4.81 us (6%)
    pallas_call x1, Pallas kernels, local(): pl.pallas_call(functools.partial(kernel, cfg), out_shape=(jax.ShapeDtypeS...  71.1 us
    unnamed x3, local copies, waits for them, and re-layouts  4.81 us

profile of v2, /device:TPU:1, one launch (start us, length us, event | category | flops | bytes accessed | tf_op | source)
XLA Modules:
  0.0 76.5 jit_solution(9807731643120219236)
XLA Ops:
  0.6 71.1 %shard_map.148 = (bf16[512,512]{1,0:T(8,128)(2,1)}, bf16[64,512]{1,0:T(8,128)(2,1)}, bf16[16,16,128]{2,1,0:T(8,128)(2,1)}) custom-call(bf16[512,896]{1,0:T(8,128)(2,1)} %hid_h.1, bf16[896,512]{1,0:T(8,128)(2,1)} %ld_h.1, bf16[64,896]{1,0:T(8,128)(2,1)} %rd_h.1, f32[1,512]{1,0:T(1,128)} %bitcast.7, s32[4]{0:T(128)} %lens.1, s32[128]{0:T(128)} %rowreq.1, ...), custom_call_target="tpu_custom_call" | custom-call | tf_op jit(solution)/shard_map/pallas_call | solution.py:499
  71.7 1.9 %copy.19 = bf16[512,512]{1,0:T(8,128)(2,1)} copy(bf16[512,512]{1,0:T(8,128)(2,1)} %get-tuple-element.12) | data formatting | bytes 1048576
  73.6 1.5 %copy.20 = bf16[64,512]{1,0:T(8,128)(2,1)} copy(bf16[64,512]{1,0:T(8,128)(2,1)} %get-tuple-element.13) | data formatting | bytes 131072
  75.1 1.5 %copy.21 = bf16[4,4,16,128]{3,2,1,0:T(8,128)(2,1)} copy(bf16[4,4,16,128]{3,2,1,0:T(8,128)(2,1)} %bitcast.6) | data formatting | bytes 131072

commit v3 on v2

--- a/solution.py
+++ b/solution.py
@@ -15,6 +15,7 @@
 Y_SIZE = 4
 CORES = 2
 LANES = 128
+LAST_AT_ONCE = 2
 AT_ONCE = 4
 F32 = jnp.float32
 BF16 = jnp.bfloat16
@@ -63,6 +64,8 @@
 
     y_order = [0, 1] + ([ny - 1] + list(range(2, ny - 1)) if ny > 2 else [])
     y_place = {d: i for i, d in enumerate(y_order)}
+    y_near = y_order[1:3]
+    y_far = y_order[3:]
 
     loads = [
         (qn_h, qn),
@@ -87,21 +90,17 @@
     for peer in peers:
         pl.semaphore_signal(barrier, inc=1, device_id=peer, device_id_type=MESH)
 
-    lane = lax.broadcasted_iota(jnp.int32, (tr, LANES), 1)
-    row_of = lax.broadcasted_iota(jnp.int32, (tr, LANES), 0) % rows
-    request = jnp.zeros((tr, LANES), jnp.int32)
-    for r in range(rows):
-        request = jnp.where(row_of == r, rowreq[ctx * rows + r], request)
-    one_hot = jnp.where(lane - rope == request, 1.0, 0.0)
-    qf[1] = jnp.zeros(qf.shape[1:], F32)
     loads[0].wait()
     loads[1].wait()
     qf[0] = qn[...].astype(F32)
     qf[1, :, :, 0:rope] = qr[...].astype(F32)
+    lane = lax.broadcasted_iota(jnp.int32, (tr, LANES), 1)
     for h in range(heads):
-        q_snd[h, :, 0:LANES] = qf[0, :, h, :].astype(BF16)
-        q_snd[h, :, LANES:] = (qf[1, :, h, :] + one_hot).astype(BF16)
-    qg[0, :, y] = q_snd[pl.ds(y * hs, hs)]
+        q_snd[h // hs, h % hs] = qf[0, :, h, :].astype(BF16)
+    for h in range(0, heads, 2):
+        pair = jnp.where(lane < rope, qf[1, :, h, :], pltpu.roll(qf[1, :, h + 1, :], rope, 1))
+        q_snd[h // hs, hs + (h % hs) // 2] = pair.astype(BF16)
+    qg[0, :, y] = q_snd[y]
     loads[6].wait()
     loads[7].wait()
     nkv[y, :, 0:lat] = nl[...].reshape(tr, lat)
@@ -121,7 +120,7 @@
     for d in range(1, ny):
         to = up(y, d, ny)
         q1.append(
-            remote(q_snd.at[pl.ds(to * hs, hs)], qg.at[0, :, y], q1_ssem.at[d], q1_rsem.at[d], y_peer[d])
+            remote(q_snd.at[to], qg.at[0, :, y], q1_ssem.at[d], q1_rsem.at[d], y_peer[d])
         )
         n1.append(remote(nkv.at[y], nkv.at[y], n1_ssem.at[d], n1_rsem.at[d], y_peer[d]))
     for copy in q1 + n1:
@@ -134,14 +133,45 @@
     for copy in q1:
         copy.wait_recv()
 
-    def z_copy(d):
-        return remote(
-            qg.at[0], qg.at[d], q2_ssem.at[d], q2_rsem.at[d], dev(up(z, d, nz), y, x, c)
+    def z_copies(step):
+        forth = remote(
+            qg.at[step - 1], qg.at[step], q2_ssem.at[0, step], q2_rsem.at[0, step], dev(up(z, 1, nz), y, x, c)
         )
+        back_slot = (nz - step + 1) % nz
+        back = remote(
+            qg.at[back_slot],
+            qg.at[nz - step],
+            q2_ssem.at[1, step],
+            q2_rsem.at[1, step],
+            dev(up(z, nz - 1, nz), y, x, c),
+        )
+        return forth, back
+
+    z_far = None
+    if nz > 1:
+        z_far = remote(
+            qg.at[0],
+            qg.at[nz // 2],
+            q2_ssem.at[0, nz // 2],
+            q2_rsem.at[0, nz // 2],
+            dev(up(z, nz // 2, nz), y, x, c),
+        )
+    z_steps = {step: z_copies(step) for step in range(1, nz // 2)}
+    z_received = set()
+
+    def z_receive(step):
+        if step in z_steps and step not in z_received:
+            z_received.add(step)
+            for copy in z_steps[step]:
+                copy.wait_recv()
+
+    def z_send(step):
+        if step in z_steps:
+            for copy in z_steps[step]:
+                copy.start()
 
     z_order = [(i + 1) // 2 if i % 2 else (nz - i // 2) % nz for i in range(nz)]
-    for d in z_order[1:]:
-        z_copy(d).start()
+    z_send(1)
 
     a_copy.wait_recv()
     part[...] += a_rcv[...].astype(F32)
@@ -149,6 +179,10 @@
     b = [remote(b_snd.at[up(x, d, nx)], b_rcv.at[d], b_ssem.at[d], b_rsem.at[d], x_peer[d]) for d in range(1, nx)]
     for copy in b:
         copy.start()
+    z_receive(1)
+    z_send(2)
+    if z_far is not None:
+        z_far.start()
 
     loads[11].wait()
     for h in range(hs):
@@ -181,9 +215,9 @@
     rotated = jnp.where(lane < rope, raw * cosine + turned * sine, penalty)
     kv[0, 0, own_rows, lat:] = rotated.astype(BF16)
 
-    def x_copy(d):
-        place = kv.at[0, 0, own_rows]
-        return remote(place, place, x_ssem.at[d], x_rsem.at[d], x_peer[d])
+    def x_copy(p, e):
+        place = kv.at[0, p, own_rows]
+        return remote(place, place, x_ssem.at[p, e], x_rsem.at[p, e], x_peer[e])
 
     def to_sibling(d):
         part_rows = pl.ds(pl.multiple_of(up(x, nx - d, nx) * sl, sl), sl)
@@ -195,37 +229,55 @@
             kv.at[0, 0, part_rows], kv.at[0, y_place[d], part_rows], y_ssem.at[d, e], y_rsem.at[d, e], y_peer[d]
         )
 
-    for d in range(1, nx):
-        x_copy(d).start()
+    for e in range(1, nx):
+        x_copy(0, e).start()
     to_sibling(0).start()
     for d in y_order[1:]:
         y_copy(d, 0).start()
+    z_receive(2)
+    z_send(3)
     for e in range(1, nx):
-        x_copy(e).wait_recv()
+        x_copy(0, e).wait_recv()
         to_sibling(e).start()
-        for d in y_order[1:]:
+        for d in y_near:
             y_copy(d, e).start()
 
     ml[...] = jnp.zeros(ml.shape, F32)
     for copy in n1:
         copy.wait_recv()
     loads[10].wait()
+    for d in y_far:
+        y_copy(d, 0).wait_recv()
+        for e in range(1, nx):
+            x_copy(y_place[d], e).start()
     for e in range(nx):
         to_sibling(e).wait_recv()
 
     def chunk_keys(pieces):
         return jnp.concatenate([kv[i, j] for i, j in pieces], axis=0)
 
-    def transpose_values(pieces):
+    def transpose_values(pieces, first=0):
         for k, (i, j) in enumerate(pieces):
-            vt[:, k * half : (k + 1) * half] = kv[i, j, :, 0:lat].T
+            vt[:, (first + k) * half : (first + k + 1) * half] = kv[i, j, :, 0:lat].T
+
+    per_head = ny * tr
+    lane = lax.broadcasted_iota(jnp.int32, (per_head, LANES), 1)
+    line = lax.broadcasted_iota(jnp.int32, (per_head, LANES), 0)
 
     def absorb(s):
-        qa[s, :, lat:] = qg[s, :, :, :, LANES:].reshape(group, LANES)
+        first_row = up(z, nz - s, nz) * (ny * rows)
+        request = jnp.zeros((per_head, LANES), jnp.int32)
+        for i in range(ny * rows):
+            here = (line // tr == i // rows) & (line % rows == i % rows)
+            request = jnp.where(here, rowreq[first_row + i], request)
+        one_hot = jnp.where(lane - rope == request, 1.0, 0.0)
         for h in range(hs):
-            qa[s, pl.ds(h * (group // hs), group // hs), 0:lat] = nn(
-                qg[s, h, :, :, 0:LANES].reshape(group // hs, LANES), ku[h]
-            ).astype(BF16)
+            here = pl.ds(h * per_head, per_head)
+            qa[s, here, 0:lat] = nn(qg[s, h].reshape(per_head, LANES), ku[h]).astype(BF16)
+            pair = qg[s, hs + h // 2].reshape(per_head, LANES).astype(F32)
+            if h % 2:
+                pair = pltpu.roll(pair, rope, 1)
+            qa[s, here, lat:] = jnp.where(lane < rope, pair, one_hot).astype(BF16)
 
     def first_keys(keys, values, slots):
         scores = [nt(keys, qa[s]) for s in slots]
@@ -262,8 +314,10 @@
     transpose_values(own_pieces)
     for slots in bunches:
         for s in slots:
-            if s:
-                z_copy(s).wait_recv()
+            if nz > 1 and s == nz // 2:
+                z_far.wait_recv()
+            elif s:
+                z_receive(min(s, nz - s))
             absorb(s)
         put(slots, *first_keys(chunk_keys(own_pieces), vt[:, 0 : CORES * half], slots))
 
@@ -289,29 +343,23 @@
     scores = jnp.where(allowed, nt(new_keys, qa[0]), MASKED)
     put([0], *next_keys([scores], new_keys[:, 0:lat].astype(F32).T.astype(BF16), [0]))
 
-    def arrive(p):
-        for e in range(nx):
-            y_copy(y_order[p], e).wait_recv()
-        copy = remote(kv.at[0, p], kv.at[1, p], s_ssem.at[p], s_rsem.at[p], sibling)
-        copy.start()
-        return copy
-
-    forwards = {}
-    chunks = []
-    if ny > 2:
-        chunks = [[(0, 1), (0, 2), (1, 1), (1, 2)]]
-    chunks += [[(0, p), (1, p)] for p in (range(3, ny) if ny > 2 else range(1, ny))]
-    for pieces in chunks[:-1]:
-        for i, p in pieces:
-            if p not in forwards:
-                forwards[p] = arrive(p)
-        for i, p in pieces:
-            if i == 1:
-                forwards[p].wait_recv()
-        transpose_values(pieces)
-        for slots in bunches:
-            keys = chunk_keys(pieces)
-            put(slots, *next_keys([nt(keys, qa[s]) for s in slots], vt[:, 0 : len(pieces) * half], slots))
+    pieces = [(i, p) for i in range(CORES) for p in range(1, ny)]
+    forwards = []
+    for p in range(1, ny):
+        d = y_order[p]
+        for e in range(1, nx):
+            if d in y_near:
+                y_copy(d, e).wait_recv()
+            else:
+                x_copy(p, e).wait_recv()
+        if d in y_near:
+            y_copy(d, 0).wait_recv()
+        forwards.append(remote(kv.at[0, p], kv.at[1, p], s_ssem.at[p], s_rsem.at[p], sibling))
+        forwards[-1].start()
+    transpose_values(pieces[: ny - 1])
+    for copy in forwards:
+        copy.wait_recv()
+    transpose_values(pieces[ny - 1 :], ny - 1)
 
     def back(s):
         to = dev(up(z, nz - s, nz), y, x, c)
@@ -320,18 +368,11 @@
             remote(ml.at[s], ml_rcv.at[s], m_ssem.at[s], m_rsem.at[s], to),
         )
 
-    pieces = chunks[-1]
-    for i, p in pieces:
-        if p not in forwards:
-            forwards[p] = arrive(p)
-    for i, p in pieces:
-        if i == 1:
-            forwards[p].wait_recv()
-    transpose_values(pieces)
     of_head = lax.broadcasted_iota(jnp.int32, (LANES, group), 1) // (group // hs)
     own_values = None
-    for slots in bunches[::-1]:
-        slots = slots[::-1]
+    last_order = z_order[::-1]
+    for i in range(0, nz, LAST_AT_ONCE):
+        slots = last_order[i : i + LAST_AT_ONCE]
         keys = chunk_keys(pieces)
         tops, sums, mixed = next_keys([nt(keys, qa[s]) for s in slots], vt[:, 0 : len(pieces) * half], slots)
         put(slots, tops, sums, [None] * len(slots))
@@ -382,21 +423,35 @@
     a_copy.wait_send()
     for copy in q1 + n1 + b + back_y:
         copy.wait_send()
-    for d in range(1, nz):
-        z_copy(d).wait_send()
-        for copy in back(d):
+    for copies in z_steps.values():
+        for copy in copies:
+            copy.wait_send()
+    if z_far is not None:
+        z_far.wait_send()
+    for s in range(1, nz):
+        for copy in back(s):
             copy.wait_send()
     for e in range(nx):
         if e:
-            x_copy(e).wait_send()
+            x_copy(0, e).wait_send()
+            for d in y_far:
+                x_copy(y_place[d], e).wait_send()
         to_sibling(e).wait_send()
-        for d in range(1, ny):
+        for d in y_near + (y_far if e == 0 else []):
             y_copy(d, e).wait_send()
-    for copy in forwards.values():
+    for copy in forwards:
         copy.wait_send()
     for copy in outs:
         copy.wait()
     hv_copy.wait()
+
+
+def place_outputs(a, b, c, a_out, b_out, c_out, sem):
+    copies = [pltpu.make_async_copy(i, o, sem.at[k]) for k, (i, o) in enumerate(((a, a_out), (b, b_out), (c, c_out)))]
+    for copy in copies:
+        copy.start()
+    for copy in copies:
+        copy.wait()
 
 
 def local(
@@ -455,11 +510,11 @@
         dma((nx,)),
         dma((nx,)),
         vmem((CORES, ny, half, wide), BF16),
-        vmem((lat, max(1, ny // 2) * tok), BF16),
+        vmem((lat, max(1, ny - 1) * tok), BF16),
         vmem((hs * LANES, lat), BF16),
         vmem((CORES, rope, half), BF16),
-        dma((nx,)),
-        dma((nx,)),
+        dma((ny, nx)),
+        dma((ny, nx)),
         dma((nx,)),
         dma((nx,)),
         dma((ny,)),
@@ -468,16 +523,16 @@
         dma((ny, nx)),
         dma((2 * CORES + 1,)),
         vmem((2, tr, heads, LANES), F32),
-        vmem((heads, tr, 2 * LANES), BF16),
-        vmem((nz, hs, ny, tr, 2 * LANES), BF16),
+        vmem((ny, hs + hs // 2, tr, LANES), BF16),
+        vmem((nz, hs + hs // 2, ny, tr, LANES), BF16),
         vmem((nz, group, wide), BF16),
         vmem((ny, tr, wide), BF16),
         dma((ny,)),
         dma((ny,)),
         dma((ny,)),
         dma((ny,)),
-        dma((nz,)),
-        dma((nz,)),
+        dma((2, nz // 2 + 1)),
+        dma((2, nz // 2 + 1)),
         vmem((nz, lat, group), F32),
         vmem((nz, 8, group), F32),
         vmem((nz, LANES, group), BF16),
@@ -524,6 +579,13 @@
         value_up,
         jnp.asarray(spare),
     )
+    latent_cache, rope_cache, head_values = pl.pallas_call(
+        place_outputs,
+        out_shape=tuple(jax.ShapeDtypeStruct(a.shape, a.dtype) for a in (latent_cache, rope_cache, head_values)),
+        in_specs=[pl.BlockSpec(memory_space=pltpu.VMEM)] * 3,
+        out_specs=(anywhere,) * 3,
+        scratch_shapes=[dma((3,))],
+    )(latent_cache, rope_cache, head_values)
     return (latent_cache, rope_cache, head_values.reshape(steps, rows, heads, LANES))
 
 

time: 77.7 us -> 60.6 us (0.78); the launches traced: 76.5 us -> 60.5 us
  Pallas kernels: 71.1 us -> 59.7 us
  local copies, waits for them, and re-layouts: 4.81 us -> 0 us
    pallas_call x1, Pallas kernels: 71.1 us -> 57.7 us  [local(): pl.pallas_call(functools.partial(kernel, cfg), out_shape=(jax.ShapeDtypeS...]
    unnamed x3 -> x0, local copies, waits for them, and re-layouts: 4.81 us -> none
    pallas_call x0 -> x1, Pallas kernels: none -> 1.93 us  [local(): pl.pallas_call(place_outputs, out_shape=tuple((jax.ShapeDtypeStruct(a.sha...]
where the time goes in v3:
time: 60.6 us; the launch traced here: 60.5 us
  Pallas kernels  59.7 us (99%)
  between operations  0.8 us (1%)
    pallas_call x1, Pallas kernels, local(): pl.pallas_call(functools.partial(kernel, cfg), out_shape=(jax.ShapeDtypeS...  57.7 us
    pallas_call x1, Pallas kernels, local(): pl.pallas_call(place_outputs, out_shape=tuple((jax.ShapeDtypeStruct(a.sha...  1.93 us

profile of v3, /device:TPU:1, one launch (start us, length us, event | category | flops | bytes accessed | tf_op | source)
XLA Modules:
  0.0 60.5 jit_solution(8633423570235389334)
XLA Ops:
  0.6 57.7 %shard_map.148 = (bf16[512,512]{1,0:T(8,128)(2,1)}, bf16[64,512]{1,0:T(8,128)(2,1)}, bf16[16,16,128]{2,1,0:T(8,128)(2,1)}) custom-call(bf16[512,896]{1,0:T(8,128)(2,1)} %hid_h.1, bf16[896,512]{1,0:T(8,128)(2,1)} %ld_h.1, bf16[64,896]{1,0:T(8,128)(2,1)} %rd_h.1, f32[1,512]{1,0:T(1,128)} %bitcast.6, s32[4]{0:T(128)} %lens.1, s32[128]{0:T(128)} %rowreq.1, ...), custom_call_target="tpu_custom_call" | custom-call | tf_op jit(solution)/shard_map/pallas_call | solution.py:554
  58.4 1.9 %shard_map.149 = (bf16[512,512]{1,0:T(8,128)(2,1)}, bf16[64,512]{1,0:T(8,128)(2,1)}, bf16[16,16,128]{2,1,0:T(8,128)(2,1)}) custom-call(bf16[512,512]{1,0:T(8,128)(2,1)} %get-tuple-element.9.a, bf16[64,512]{1,0:T(8,128)(2,1)} %get-tuple-element.10.b, bf16[16,16,128]{2,1,0:T(8,128)(2,1)} %get-tuple-element.11.c), custom_call_target="tpu_custom_call" | custom-call | tf_op jit(solution)/shard_map/pallas_call | solution.py:582

commit v4 on v3

--- a/solution.py
+++ b/solution.py
@@ -15,7 +15,10 @@
 Y_SIZE = 4
 CORES = 2
 LANES = 128
+CUTS = 2
 LAST_AT_ONCE = 2
+PART = 2
+JOIN = 2
 AT_ONCE = 4
 F32 = jnp.float32
 BF16 = jnp.bfloat16
@@ -176,9 +179,16 @@
     a_copy.wait_recv()
     part[...] += a_rcv[...].astype(F32)
     b_snd[...] = part[...].astype(BF16).reshape(nx, sl, wide)
-    b = [remote(b_snd.at[up(x, d, nx)], b_rcv.at[d], b_ssem.at[d], b_rsem.at[d], x_peer[d]) for d in range(1, nx)]
-    for copy in b:
-        copy.start()
+    cut = sl // CUTS
+    x_order = ([1, nx - 1] + list(range(2, nx - 1))) if nx > 2 else list(range(1, nx))
+    b = {}
+    for u in range(CUTS):
+        for d in x_order:
+            rows_u = pl.ds(u * cut, cut)
+            b[d, u] = remote(
+                b_snd.at[up(x, d, nx), rows_u], b_rcv.at[d, rows_u], b_ssem.at[d, u], b_rsem.at[d, u], x_peer[d]
+            )
+            b[d, u].start()
     z_receive(1)
     z_send(2)
     if z_far is not None:
@@ -202,56 +212,62 @@
     lane = lax.broadcasted_iota(jnp.int32, (sl, LANES), 1)
     penalty = jnp.where((lane >= rope) & (lane < rope + lens.shape[0]) & (lane - rope != owner), MASKED, 0.0)
 
-    own_rows = pl.ds(pl.multiple_of(x * sl, sl), sl)
-    total = part[own_rows, :]
-    for d in range(1, nx):
-        b[d - 1].wait_recv()
-        total = total + b_rcv[d].astype(F32)
-    latent = total[:, 0:lat]
-    mean_square = jnp.mean(latent * latent, axis=-1, keepdims=True)
-    kv[0, 0, own_rows, 0:lat] = (latent * lax.rsqrt(mean_square + EPSILON) * gain[...]).astype(BF16)
-    raw = total[:, lat:]
-    turned = jnp.where(lane < rope // 2, -pltpu.roll(raw, LANES - rope // 2, 1), pltpu.roll(raw, rope // 2, 1))
-    rotated = jnp.where(lane < rope, raw * cosine + turned * sine, penalty)
-    kv[0, 0, own_rows, lat:] = rotated.astype(BF16)
-
-    def x_copy(p, e):
-        place = kv.at[0, p, own_rows]
-        return remote(place, place, x_ssem.at[p, e], x_rsem.at[p, e], x_peer[e])
-
-    def to_sibling(d):
-        part_rows = pl.ds(pl.multiple_of(up(x, nx - d, nx) * sl, sl), sl)
-        return remote(kv.at[0, 0, part_rows], kv.at[1, 0, part_rows], s0_ssem.at[d], s0_rsem.at[d], sibling)
-
-    def y_copy(d, e):
-        part_rows = pl.ds(pl.multiple_of(up(x, nx - e, nx) * sl, sl), sl)
+    def rows_of(e, u):
+        return pl.ds(pl.multiple_of(up(x, nx - e, nx) * sl + u * cut, cut), cut)
+
+    def x_copy(p, e, u):
+        place = kv.at[0, p, rows_of(0, u)]
+        return remote(place, place, x_ssem.at[p, e, u], x_rsem.at[p, e, u], x_peer[e])
+
+    def to_sibling(e, u):
+        there = rows_of(e, u)
+        return remote(kv.at[0, 0, there], kv.at[1, 0, there], s0_ssem.at[e, u], s0_rsem.at[e, u], sibling)
+
+    def y_copy(d, e, u):
+        there = rows_of(e, u)
         return remote(
-            kv.at[0, 0, part_rows], kv.at[0, y_place[d], part_rows], y_ssem.at[d, e], y_rsem.at[d, e], y_peer[d]
+            kv.at[0, 0, there], kv.at[0, y_place[d], there], y_ssem.at[d, e, u], y_rsem.at[d, e, u], y_peer[d]
         )
 
-    for e in range(1, nx):
-        x_copy(0, e).start()
-    to_sibling(0).start()
-    for d in y_order[1:]:
-        y_copy(d, 0).start()
+    for u in range(CUTS):
+        some = slice(u * cut, (u + 1) * cut)
+        total = part[rows_of(0, u), :]
+        for d in x_order:
+            b[d, u].wait_recv()
+            total = total + b_rcv[d, some].astype(F32)
+        latent = total[:, 0:lat]
+        mean_square = jnp.mean(latent * latent, axis=-1, keepdims=True)
+        kv[0, 0, rows_of(0, u), 0:lat] = (latent * lax.rsqrt(mean_square + EPSILON) * gain[...]).astype(BF16)
+        raw = total[:, lat:]
+        low = lane[some] < rope // 2
+        turned = jnp.where(low, -pltpu.roll(raw, LANES - rope // 2, 1), pltpu.roll(raw, rope // 2, 1))
+        rotated = jnp.where(lane[some] < rope, raw * cosine[some] + turned * sine[some], penalty[some])
+        kv[0, 0, rows_of(0, u), lat:] = rotated.astype(BF16)
+        for e in x_order:
+            x_copy(0, e, u).start()
+        to_sibling(0, u).start()
+        for d in y_order[1:]:
+            y_copy(d, 0, u).start()
     z_receive(2)
     z_send(3)
-    for e in range(1, nx):
-        x_copy(0, e).wait_recv()
-        to_sibling(e).start()
-        for d in y_near:
-            y_copy(d, e).start()
+    for u in range(CUTS):
+        for e in x_order:
+            x_copy(0, e, u).wait_recv()
+            for d in y_near:
+                y_copy(d, e, u).start()
+            to_sibling(e, u).start()
+        for d in y_far:
+            y_copy(d, 0, u).wait_recv()
+            for e in x_order:
+                x_copy(y_place[d], e, u).start()
 
     ml[...] = jnp.zeros(ml.shape, F32)
     for copy in n1:
         copy.wait_recv()
     loads[10].wait()
-    for d in y_far:
-        y_copy(d, 0).wait_recv()
-        for e in range(1, nx):
-            x_copy(y_place[d], e).start()
-    for e in range(nx):
-        to_sibling(e).wait_recv()
+    for u in range(CUTS):
+        for e in range(nx):
+            to_sibling(e, u).wait_recv()
 
     def chunk_keys(pieces):
         return jnp.concatenate([kv[i, j] for i, j in pieces], axis=0)
@@ -279,17 +295,28 @@
                 pair = pltpu.roll(pair, rope, 1)
             qa[s, here, lat:] = jnp.where(lane < rope, pair, one_hot).astype(BF16)
 
-    def first_keys(keys, values, slots):
-        scores = [nt(keys, qa[s]) for s in slots]
+    def joined(slots):
+        return [slots[i : i + JOIN] for i in range(0, len(slots), JOIN)]
+
+    def beside(ref, slots, row=None):
+        parts = [ref[s] if row is None else ref[s, row : row + 1, :] for s in slots]
+        return parts[0] if len(parts) == 1 else jnp.concatenate(parts, axis=1)
+
+    def scores_of(keys, slots):
+        parts = [qa[s] for s in slots]
+        return nt(keys, parts[0] if len(parts) == 1 else jnp.concatenate(parts, axis=0))
+
+    def first_keys(keys, values, bunch):
+        scores = [scores_of(keys, slots) for slots in bunch]
         tops = [jnp.max(score, axis=0, keepdims=True) for score in scores]
         weights = [jnp.exp2((score - top) * scale) for score, top in zip(scores, tops)]
         sums = [jnp.sum(weight, axis=0, keepdims=True) for weight in weights]
         mixed = [nn(values, weight.astype(BF16)) for weight in weights]
         return tops, sums, mixed
 
-    def next_keys(scores, values, slots):
-        before = [ml[s, 0:1, :] for s in slots]
-        sums = [ml[s, 1:2, :] for s in slots]
+    def next_keys(scores, values, bunch):
+        before = [beside(ml, slots, 0) for slots in bunch]
+        sums = [beside(ml, slots, 1) for slots in bunch]
         tops = [jnp.maximum(old, jnp.max(score, axis=0, keepdims=True)) for old, score in zip(before, scores)]
         weights = [jnp.exp2((score - top) * scale) for score, top in zip(scores, tops)]
         keeps = [jnp.exp2((old - top) * scale) for old, top in zip(before, tops)]
@@ -297,16 +324,19 @@
             old * keep + jnp.sum(weight, axis=0, keepdims=True) for old, keep, weight in zip(sums, keeps, weights)
         ]
         mixed = [
-            ot[s] * keep + nn(values, weight.astype(BF16)) for s, keep, weight in zip(slots, keeps, weights)
+            beside(ot, slots) * keep + nn(values, weight.astype(BF16))
+            for slots, keep, weight in zip(bunch, keeps, weights)
         ]
         return tops, sums, mixed
 
-    def put(slots, tops, sums, mixed):
-        for s, top, total, mix in zip(slots, tops, sums, mixed):
-            ml[s, 0:1, :] = top
-            ml[s, 1:2, :] = total
-            if mix is not None:
-                ot[s] = mix
+    def put(bunch, tops, sums, mixed):
+        for slots, top, total, mix in zip(bunch, tops, sums, mixed):
+            for k, s in enumerate(slots):
+                here = slice(k * group, (k + 1) * group)
+                ml[s, 0:1, :] = top[:, here]
+                ml[s, 1:2, :] = total[:, here]
+                if mix is not None:
+                    ot[s] = mix[:, here]
 
     at_once = min(AT_ONCE, nz)
     bunches = [z_order[i : i + at_once] for i in range(0, nz, at_once)]
@@ -319,7 +349,8 @@
             elif s:
                 z_receive(min(s, nz - s))
             absorb(s)
-        put(slots, *first_keys(chunk_keys(own_pieces), vt[:, 0 : CORES * half], slots))
+        bunch = joined(slots)
+        put(bunch, *first_keys(chunk_keys(own_pieces), vt[:, 0 : CORES * half], bunch))
 
     sides = [c, 1 - c]
     outs = []
@@ -341,19 +372,20 @@
         & ((key_of % tr) // rows <= (query_of % tr) // rows)
     )
     scores = jnp.where(allowed, nt(new_keys, qa[0]), MASKED)
-    put([0], *next_keys([scores], new_keys[:, 0:lat].astype(F32).T.astype(BF16), [0]))
+    put([[0]], *next_keys([scores], new_keys[:, 0:lat].astype(F32).T.astype(BF16), [[0]]))
 
     pieces = [(i, p) for i in range(CORES) for p in range(1, ny)]
     forwards = []
     for p in range(1, ny):
         d = y_order[p]
-        for e in range(1, nx):
+        for u in range(CUTS):
+            for e in range(1, nx):
+                if d in y_near:
+                    y_copy(d, e, u).wait_recv()
+                else:
+                    x_copy(p, e, u).wait_recv()
             if d in y_near:
-                y_copy(d, e).wait_recv()
-            else:
-                x_copy(p, e).wait_recv()
-        if d in y_near:
-            y_copy(d, 0).wait_recv()
+                y_copy(d, 0, u).wait_recv()
         forwards.append(remote(kv.at[0, p], kv.at[1, p], s_ssem.at[p], s_rsem.at[p], sibling))
         forwards[-1].start()
     transpose_values(pieces[: ny - 1])
@@ -365,26 +397,47 @@
         to = dev(up(z, nz - s, nz), y, x, c)
         return (
             remote(u_snd.at[s], u_rcv.at[s], u_ssem.at[s], u_rsem.at[s], to),
-            remote(ml.at[s], ml_rcv.at[s], m_ssem.at[s], m_rsem.at[s], to),
+            remote(ml.at[s, pl.ds(0, 2)], ml_rcv.at[s, pl.ds(0, 2)], m_ssem.at[s], m_rsem.at[s], to),
         )
 
     of_head = lax.broadcasted_iota(jnp.int32, (LANES, group), 1) // (group // hs)
     own_values = None
     last_order = z_order[::-1]
-    for i in range(0, nz, LAST_AT_ONCE):
-        slots = last_order[i : i + LAST_AT_ONCE]
-        keys = chunk_keys(pieces)
-        tops, sums, mixed = next_keys([nt(keys, qa[s]) for s in slots], vt[:, 0 : len(pieces) * half], slots)
-        put(slots, tops, sums, [None] * len(slots))
-        for s, mix in zip(slots, mixed):
+    if nz == 8:
+        last_order = [3, 5, 4, 6, 2, 7, 1, 0]
+    turns = [last_order[i : i + LAST_AT_ONCE] for i in range(0, nz, LAST_AT_ONCE)]
+    key_parts = [chunk_keys(pieces[k : k + PART]) for k in range(0, len(pieces), PART)]
+    scores = [scores_of(keys, turns[0]) for keys in key_parts]
+    for turn, slots in enumerate(turns):
+        before = beside(ml, slots, 0)
+        top = before
+        for score in scores:
+            top = jnp.maximum(top, jnp.max(score, axis=0, keepdims=True))
+        keep = jnp.exp2((before - top) * scale)
+        total = beside(ml, slots, 1) * keep
+        mix = beside(ot, slots) * keep
+        weights, following = [], []
+        for k, score in enumerate(scores):
+            if turn + 1 < len(turns):
+                following.append(scores_of(key_parts[k], turns[turn + 1]))
+            weight = jnp.exp2((score - top) * scale)
+            total = total + jnp.sum(weight, axis=0, keepdims=True)
+            weights.append(weight.astype(BF16))
+        weights = weights[0] if len(weights) == 1 else jnp.concatenate(weights, axis=0)
+        mix = mix + nn(vt[:, 0 : len(pieces) * half], weights)
+        scores = following
+        put([slots], [top], [total], [None])
+        for some, mix in [(slots, mix)]:
             every = nn(vut[...], mix.astype(BF16))
-            values = every[0:LANES]
-            for h in range(1, hs):
-                values = jnp.where(of_head == h, every[h * LANES : (h + 1) * LANES], values)
-            if s:
-                u_snd[s] = values.astype(BF16)
-            else:
-                own_values = values
+            for k, s in enumerate(some):
+                mine = every[:, k * group : (k + 1) * group]
+                values = mine[0:LANES]
+                for h in range(1, hs):
+                    values = jnp.where(of_head == h, mine[h * LANES : (h + 1) * LANES], values)
+                if s:
+                    u_snd[s] = values.astype(BF16)
+                else:
+                    own_values = values
         for s in slots:
             if s:
                 for copy in back(s):
@@ -421,7 +474,7 @@
     hv_copy.start()
 
     a_copy.wait_send()
-    for copy in q1 + n1 + b + back_y:
+    for copy in q1 + n1 + list(b.values()) + back_y:
         copy.wait_send()
     for copies in z_steps.values():
         for copy in copies:
@@ -431,14 +484,14 @@
     for s in range(1, nz):
         for copy in back(s):
             copy.wait_send()
-    for e in range(nx):
+    for e, u in [(e, u) for e in range(nx) for u in range(CUTS)]:
         if e:
-            x_copy(0, e).wait_send()
+            x_copy(0, e, u).wait_send()
             for d in y_far:
-                x_copy(y_place[d], e).wait_send()
-        to_sibling(e).wait_send()
+                x_copy(y_place[d], e, u).wait_send()
+        to_sibling(e, u).wait_send()
         for d in y_near + (y_far if e == 0 else []):
-            y_copy(d, e).wait_send()
+            y_copy(d, e, u).wait_send()
     for copy in forwards:
         copy.wait_send()
     for copy in outs:
@@ -507,20 +560,20 @@
         vmem((nx, sl, wide), BF16),
         vmem((nx, sl, wide), BF16),
         dma((2,)),
-        dma((nx,)),
-        dma((nx,)),
+        dma((nx, CUTS)),
+        dma((nx, CUTS)),
         vmem((CORES, ny, half, wide), BF16),
         vmem((lat, max(1, ny - 1) * tok), BF16),
         vmem((hs * LANES, lat), BF16),
         vmem((CORES, rope, half), BF16),
-        dma((ny, nx)),
-        dma((ny, nx)),
-        dma((nx,)),
-        dma((nx,)),
-        dma((ny,)),
-        dma((ny,)),
-        dma((ny, nx)),
-        dma((ny, nx)),
+        dma((ny, nx, CUTS)),
+        dma((ny, nx, CUTS)),
+        dma((nx, CUTS)),
+        dma((nx, CUTS)),
+        dma((ny,)),
+        dma((ny,)),
+        dma((ny, nx, CUTS)),
+        dma((ny, nx, CUTS)),
         dma((2 * CORES + 1,)),
         vmem((2, tr, heads, LANES), F32),
         vmem((ny, hs + hs // 2, tr, LANES), BF16),

time: 60.6 us -> 60.7 us (level)
  no operation moved by 1% of the time
where the time goes in v4:
time: 60.7 us; the launch traced here: 60.6 us
  Pallas kernels  59.8 us (99%)
  between operations  0.8 us (1%)
    pallas_call x1, Pallas kernels, local(): pl.pallas_call(functools.partial(kernel, cfg), out_shape=(jax.ShapeDtypeS...  57.8 us
    pallas_call x1, Pallas kernels, local(): pl.pallas_call(place_outputs, out_shape=tuple((jax.ShapeDtypeStruct(a.sha...  1.93 us

profile of v4, /device:TPU:1, one launch (start us, length us, event | category | flops | bytes accessed | tf_op | source)
XLA Modules:
  0.0 60.6 jit_solution(8893543813417592498)
XLA Ops:
  0.6 57.8 %shard_map.148 = (bf16[512,512]{1,0:T(8,128)(2,1)}, bf16[64,512]{1,0:T(8,128)(2,1)}, bf16[16,16,128]{2,1,0:T(8,128)(2,1)}) custom-call(bf16[512,896]{1,0:T(8,128)(2,1)} %hid_h.1, bf16[896,512]{1,0:T(8,128)(2,1)} %ld_h.1, bf16[64,896]{1,0:T(8,128)(2,1)} %rd_h.1, f32[1,512]{1,0:T(1,128)} %bitcast.6, s32[4]{0:T(128)} %lens.1, s32[128]{0:T(128)} %rowreq.1, ...), custom_call_target="tpu_custom_call" | custom-call | tf_op jit(solution)/shard_map/pallas_call | solution.py:607
  58.5 1.9 %shard_map.149 = (bf16[512,512]{1,0:T(8,128)(2,1)}, bf16[64,512]{1,0:T(8,128)(2,1)}, bf16[16,16,128]{2,1,0:T(8,128)(2,1)}) custom-call(bf16[512,512]{1,0:T(8,128)(2,1)} %get-tuple-element.9.a, bf16[64,512]{1,0:T(8,128)(2,1)} %get-tuple-element.10.b, bf16[16,16,128]{2,1,0:T(8,128)(2,1)} %get-tuple-element.11.c), custom_call_target="tpu_custom_call" | custom-call | tf_op jit(solution)/shard_map/pallas_call | solution.py:635

commit v5 on v4

--- a/solution.py
+++ b/solution.py
@@ -103,7 +103,7 @@
     for h in range(0, heads, 2):
         pair = jnp.where(lane < rope, qf[1, :, h, :], pltpu.roll(qf[1, :, h + 1, :], rope, 1))
         q_snd[h // hs, hs + (h % hs) // 2] = pair.astype(BF16)
-    qg[0, :, y] = q_snd[y]
+    qg[0, y] = q_snd[y]
     loads[6].wait()
     loads[7].wait()
     nkv[y, :, 0:lat] = nl[...].reshape(tr, lat)
@@ -123,58 +123,29 @@
     for d in range(1, ny):
         to = up(y, d, ny)
         q1.append(
-            remote(q_snd.at[to], qg.at[0, :, y], q1_ssem.at[d], q1_rsem.at[d], y_peer[d])
+            remote(q_snd.at[to], qg.at[0, y], q1_ssem.at[d], q1_rsem.at[d], y_peer[d])
         )
         n1.append(remote(nkv.at[y], nkv.at[y], n1_ssem.at[d], n1_rsem.at[d], y_peer[d]))
-    for copy in q1 + n1:
+    z_order = [(i + 1) // 2 if i % 2 else (nz - i // 2) % nz for i in range(nz)]
+
+    def z_copy(d, k):
+        source = up(y, ny - d, ny)
+        return remote(
+            qg.at[0, source],
+            qg.at[k, source],
+            q2_ssem.at[d, k],
+            q2_rsem.at[d, k],
+            dev(up(z, k, nz), y, x, c),
+        )
+
+    for copy in q1:
         copy.start()
+    for k in z_order[1:]:
+        z_copy(0, k).start()
 
     loads[5].wait()
     part[:, 0:lat] = nn(hid[1], ld[...])
     part[:, lat:] = nt(hid[1], rd[...])
-
-    for copy in q1:
-        copy.wait_recv()
-
-    def z_copies(step):
-        forth = remote(
-            qg.at[step - 1], qg.at[step], q2_ssem.at[0, step], q2_rsem.at[0, step], dev(up(z, 1, nz), y, x, c)
-        )
-        back_slot = (nz - step + 1) % nz
-        back = remote(
-            qg.at[back_slot],
-            qg.at[nz - step],
-            q2_ssem.at[1, step],
-            q2_rsem.at[1, step],
-            dev(up(z, nz - 1, nz), y, x, c),
-        )
-        return forth, back
-
-    z_far = None
-    if nz > 1:
-        z_far = remote(
-            qg.at[0],
-            qg.at[nz // 2],
-            q2_ssem.at[0, nz // 2],
-            q2_rsem.at[0, nz // 2],
-            dev(up(z, nz // 2, nz), y, x, c),
-        )
-    z_steps = {step: z_copies(step) for step in range(1, nz // 2)}
-    z_received = set()
-
-    def z_receive(step):
-        if step in z_steps and step not in z_received:
-            z_received.add(step)
-            for copy in z_steps[step]:
-                copy.wait_recv()
-
-    def z_send(step):
-        if step in z_steps:
-            for copy in z_steps[step]:
-                copy.start()
-
-    z_order = [(i + 1) // 2 if i % 2 else (nz - i // 2) % nz for i in range(nz)]
-    z_send(1)
 
     a_copy.wait_recv()
     part[...] += a_rcv[...].astype(F32)
@@ -189,10 +160,12 @@
                 b_snd.at[up(x, d, nx), rows_u], b_rcv.at[d, rows_u], b_ssem.at[d, u], b_rsem.at[d, u], x_peer[d]
             )
             b[d, u].start()
-    z_receive(1)
-    z_send(2)
-    if z_far is not None:
-        z_far.start()
+    for copy in n1:
+        copy.start()
+    for d in range(1, ny):
+        q1[d - 1].wait_recv()
+        for k in z_order[1:]:
+            z_copy(d, k).start()
 
     loads[11].wait()
     for h in range(hs):
@@ -248,8 +221,6 @@
         to_sibling(0, u).start()
         for d in y_order[1:]:
             y_copy(d, 0, u).start()
-    z_receive(2)
-    z_send(3)
     for u in range(CUTS):
         for e in x_order:
             x_copy(0, e, u).wait_recv()
@@ -289,8 +260,8 @@
         one_hot = jnp.where(lane - rope == request, 1.0, 0.0)
         for h in range(hs):
             here = pl.ds(h * per_head, per_head)
-            qa[s, here, 0:lat] = nn(qg[s, h].reshape(per_head, LANES), ku[h]).astype(BF16)
-            pair = qg[s, hs + h // 2].reshape(per_head, LANES).astype(F32)
+            qa[s, here, 0:lat] = nn(qg[s, :, h].reshape(per_head, LANES), ku[h]).astype(BF16)
+            pair = qg[s, :, hs + h // 2].reshape(per_head, LANES).astype(F32)
             if h % 2:
                 pair = pltpu.roll(pair, rope, 1)
             qa[s, here, lat:] = jnp.where(lane < rope, pair, one_hot).astype(BF16)
@@ -344,10 +315,9 @@
     transpose_values(own_pieces)
     for slots in bunches:
         for s in slots:
-            if nz > 1 and s == nz // 2:
-                z_far.wait_recv()
-            elif s:
-                z_receive(min(s, nz - s))
+            if s:
+                for d in range(ny):
+                    z_copy(d, s).wait_recv()
             absorb(s)
         bunch = joined(slots)
         put(bunch, *first_keys(chunk_keys(own_pieces), vt[:, 0 : CORES * half], bunch))
@@ -476,11 +446,9 @@
     a_copy.wait_send()
     for copy in q1 + n1 + list(b.values()) + back_y:
         copy.wait_send()
-    for copies in z_steps.values():
-        for copy in copies:
-            copy.wait_send()
-    if z_far is not None:
-        z_far.wait_send()
+    for k in range(1, nz):
+        for d in range(ny):
+            z_copy(d, k).wait_send()
     for s in range(1, nz):
         for copy in back(s):
             copy.wait_send()
@@ -577,15 +545,15 @@
         dma((2 * CORES + 1,)),
         vmem((2, tr, heads, LANES), F32),
         vmem((ny, hs + hs // 2, tr, LANES), BF16),
-        vmem((nz, hs + hs // 2, ny, tr, LANES), BF16),
+        vmem((nz, ny, hs + hs // 2, tr, LANES), BF16),
         vmem((nz, group, wide), BF16),
         vmem((ny, tr, wide), BF16),
         dma((ny,)),
         dma((ny,)),
         dma((ny,)),
         dma((ny,)),
-        dma((2, nz // 2 + 1)),
-        dma((2, nz // 2 + 1)),
+        dma((ny, nz)),
+        dma((ny, nz)),
         vmem((nz, lat, group), F32),
         vmem((nz, 8, group), F32),
         vmem((nz, LANES, group), BF16),

time: 60.7 us -> 61.5 us (1.013)
  no operation moved by 1% of the time
where the time goes in v5:
time: 61.5 us; the launch traced here: 61 us
  Pallas kernels  60.2 us (98%)
  between operations  0.8 us (1%)
    pallas_call x1, Pallas kernels, local(): pl.pallas_call(functools.partial(kernel, cfg), out_shape=(jax.ShapeDtypeS...  58.3 us
    pallas_call x1, Pallas kernels, local(): pl.pallas_call(place_outputs, out_shape=tuple((jax.ShapeDtypeStruct(a.sha...  1.93 us

profile of v5, /device:TPU:1, one launch (start us, length us, event | category | flops | bytes accessed | tf_op | source)
XLA Modules:
  0.0 61.0 jit_solution(17581148520805700268)
XLA Ops:
  0.6 58.3 %shard_map.148 = (bf16[512,512]{1,0:T(8,128)(2,1)}, bf16[64,512]{1,0:T(8,128)(2,1)}, bf16[16,16,128]{2,1,0:T(8,128)(2,1)}) custom-call(bf16[512,896]{1,0:T(8,128)(2,1)} %hid_h.1, bf16[896,512]{1,0:T(8,128)(2,1)} %ld_h.1, bf16[64,896]{1,0:T(8,128)(2,1)} %rd_h.1, f32[1,512]{1,0:T(1,128)} %bitcast.6, s32[4]{0:T(128)} %lens.1, s32[128]{0:T(128)} %rowreq.1, ...), custom_call_target="tpu_custom_call" | custom-call | tf_op jit(solution)/shard_map/pallas_call | solution.py:575
  58.9 1.9 %shard_map.149 = (bf16[512,512]{1,0:T(8,128)(2,1)}, bf16[64,512]{1,0:T(8,128)(2,1)}, bf16[16,16,128]{2,1,0:T(8,128)(2,1)}) custom-call(bf16[512,512]{1,0:T(8,128)(2,1)} %get-tuple-element.9.a, bf16[64,512]{1,0:T(8,128)(2,1)} %get-tuple-element.10.b, bf16[16,16,128]{2,1,0:T(8,128)(2,1)} %get-tuple-element.11.c), custom_call_target="tpu_custom_call" | custom-call | tf_op jit(solution)/shard_map/pallas_call | solution.py:603

commit v6 on v5

--- a/solution.py
+++ b/solution.py
@@ -38,7 +38,7 @@
     lat_o, rope_o, hv_o,
     hid, ld, rd, gain, qn, qr, nl, nr, ku, vu, freq, loc,
     a_snd, a_rcv, part, b_snd, b_rcv, a_sem, b_ssem, b_rsem,
-    kv, vt, vut, rope_t, x_ssem, x_rsem, s0_ssem, s0_rsem, s_ssem, s_rsem, y_ssem, y_rsem, o_sem,
+    kv, vt, vt_own, vut, rope_t, x_ssem, x_rsem, s0_ssem, s0_rsem, s_ssem, s_rsem, y_ssem, y_rsem, o_sem,
     qf, q_snd, qg, qa, nkv, q1_ssem, q1_rsem, n1_ssem, n1_rsem, q2_ssem, q2_rsem,
     ot, ml, u_snd, u_rcv, ml_rcv, u_ssem, u_rsem, m_ssem, m_rsem,
     o_snd, o_rcv, of, hv, h_ssem, h_rsem,
@@ -312,15 +312,19 @@
     at_once = min(AT_ONCE, nz)
     bunches = [z_order[i : i + at_once] for i in range(0, nz, at_once)]
     own_pieces = [(0, 0), (1, 0)]
-    transpose_values(own_pieces)
-    for slots in bunches:
+    for i, j in own_pieces:
+        vt_own[:, i * half : (i + 1) * half] = kv[i, j, :, 0:lat].T
+
+    def visit_own(slots):
         for s in slots:
             if s:
                 for d in range(ny):
                     z_copy(d, s).wait_recv()
             absorb(s)
         bunch = joined(slots)
-        put(bunch, *first_keys(chunk_keys(own_pieces), vt[:, 0 : CORES * half], bunch))
+        put(bunch, *first_keys(chunk_keys(own_pieces), vt_own[...], bunch))
+
+    visit_own(bunches[0])
 
     sides = [c, 1 - c]
     outs = []
@@ -358,6 +362,8 @@
                 y_copy(d, 0, u).wait_recv()
         forwards.append(remote(kv.at[0, p], kv.at[1, p], s_ssem.at[p], s_rsem.at[p], sibling))
         forwards[-1].start()
+    for slots in bunches[1:]:
+        visit_own(slots)
     transpose_values(pieces[: ny - 1])
     for copy in forwards:
         copy.wait_recv()
@@ -426,15 +432,17 @@
         numerator = numerator + u_rcv[s].astype(F32) * keep
         denominator = denominator + ml_rcv[s, 1:2, :] * keep
     values = (numerator / denominator).T.astype(BF16)
-    o_snd[...] = values.reshape(hs, ny, tr, LANES)
+    values = values.reshape(hs, ny, tr, LANES)
+    for i in range(ny):
+        o_snd[i] = values[:, i]
     own_heads = pl.ds(y * hs, hs)
     back_y = [
-        remote(o_snd.at[:, up(y, d, ny)], o_rcv.at[own_heads], h_ssem.at[d], h_rsem.at[d], y_peer[d])
+        remote(o_snd.at[up(y, d, ny)], o_rcv.at[own_heads], h_ssem.at[d], h_rsem.at[d], y_peer[d])
         for d in range(1, ny)
     ]
     for copy in back_y:
         copy.start()
-    o_rcv[own_heads] = o_snd[:, y]
+    o_rcv[own_heads] = o_snd[y]
     for copy in back_y:
         copy.wait_recv()
     for h in range(heads):
@@ -532,6 +540,7 @@
         dma((nx, CUTS)),
         vmem((CORES, ny, half, wide), BF16),
         vmem((lat, max(1, ny - 1) * tok), BF16),
+        vmem((lat, tok), BF16),
         vmem((hs * LANES, lat), BF16),
         vmem((CORES, rope, half), BF16),
         dma((ny, nx, CUTS)),
@@ -563,7 +572,7 @@
         dma((nz,)),
         dma((nz,)),
         dma((nz,)),
-        vmem((hs, ny, tr, LANES), BF16),
+        vmem((ny, hs, tr, LANES), BF16),
         vmem((heads, tr, LANES), BF16),
         vmem((tr, heads, LANES), F32),
         vmem((tr, heads, LANES), BF16),

time: 61.5 us -> 59.9 us (0.974)
  Pallas kernels: 60.2 us -> 59 us
    pallas_call x1, Pallas kernels: 58.3 us -> 57.1 us  [local(): pl.pallas_call(functools.partial(kernel, cfg), out_shape=(jax.ShapeDtypeS...]
where the time goes in v6:
time: 59.9 us; the launch traced here: 59.8 us
  Pallas kernels  59 us (98%)
  between operations  0.8 us (1%)
    pallas_call x1, Pallas kernels, local(): pl.pallas_call(functools.partial(kernel, cfg), out_shape=(jax.ShapeDtypeS...  57.1 us
    pallas_call x1, Pallas kernels, local(): pl.pallas_call(place_outputs, out_shape=tuple((jax.ShapeDtypeStruct(a.sha...  1.93 us

profile of v6, /device:TPU:1, one launch (start us, length us, event | category | flops | bytes accessed | tf_op | source)
XLA Modules:
  0.0 59.8 jit_solution(13953782361957091266)
XLA Ops:
  0.6 57.1 %shard_map.148 = (bf16[512,512]{1,0:T(8,128)(2,1)}, bf16[64,512]{1,0:T(8,128)(2,1)}, bf16[16,16,128]{2,1,0:T(8,128)(2,1)}) custom-call(bf16[512,896]{1,0:T(8,128)(2,1)} %hid_h.1, bf16[896,512]{1,0:T(8,128)(2,1)} %ld_h.1, bf16[64,896]{1,0:T(8,128)(2,1)} %rd_h.1, f32[1,512]{1,0:T(1,128)} %bitcast.6, s32[4]{0:T(128)} %lens.1, s32[128]{0:T(128)} %rowreq.1, ...), custom_call_target="tpu_custom_call" | custom-call | tf_op jit(solution)/shard_map/pallas_call | solution.py:584
  57.7 1.9 %shard_map.149 = (bf16[512,512]{1,0:T(8,128)(2,1)}, bf16[64,512]{1,0:T(8,128)(2,1)}, bf16[16,16,128]{2,1,0:T(8,128)(2,1)}) custom-call(bf16[512,512]{1,0:T(8,128)(2,1)} %get-tuple-element.9.a, bf16[64,512]{1,0:T(8,128)(2,1)} %get-tuple-element.10.b, bf16[16,16,128]{2,1,0:T(8,128)(2,1)} %get-tuple-element.11.c), custom_call_target="tpu_custom_call" | custom-call | tf_op jit(solution)/shard_map/pallas_call | solution.py:612
